TPU v7x, 128 devices: a whole 4x4x4 slice. The times are simulated.
128 devices in a mesh: win: 4 (over y_lo, core), blk: 32 (over y_hi, z, x).
Axes of the slice: x: 4, y: 4 (y_hi: 2, y_lo: 2; y = y_hi * 2 + y_lo), z: 4, core: 2. Of those that a mesh axis runs over, the one named last changes fastest.
Arguments:
- hidden_in: bfloat16 [4, 8192, 1920], P('win', 'blk'), may hold values from -6 to 6
- cond_codes: int32 [4, 2048], P('win', 'blk'), may hold values from 0 to 2047
- level_ids: int32 [4], P('win'), may hold values from 0 to 1, as said below
- qkv_weight: bfloat16 [1920, 1440], P(('win', 'blk')), may hold values from -0.125 to 0.125
- attn_out_weight: bfloat16 [480, 1920], P(None, ('win', 'blk')), may hold values from -1 to 1
- mlp_in_weight: bfloat16 [1920, 1920], P(('win', 'blk')), may hold values from -0.125 to 0.125
- mlp_out_weight: bfloat16 [1920, 1920], P(('win', 'blk')), may hold values from -0.125 to 0.125
- code_table: bfloat16 [2048, 1920], P(('win', 'blk')), may hold values from -6 to 6
- level_table: bfloat16 [2, 1920], P(None, ('win', 'blk')), may hold values from -6 to 6
- norm_gain: bfloat16 [2, 1920], P(None, ('win', 'blk')), may hold values from 0.5 to 2
- norm_bias: bfloat16 [2, 1920], P(None, ('win', 'blk')), may hold values from -0.5 to 0.5
- grad_out: bfloat16 [4, 8192, 1920], P('win', 'blk'), may hold values from -6 to 6
Outputs:
- block_out: bfloat16 [4, 8192, 1920], P('win', 'blk')
- grad_in: float32 [4, 8192, 1920], P('win', 'blk')
- grad_qkv: float32 [1920, 1440], P(('win', 'blk'))
- grad_attn_out: float32 [480, 1920], P(None, ('win', 'blk'))
- grad_mlp_in: float32 [1920, 1920], P(('win', 'blk'))
- grad_mlp_out: float32 [1920, 1920], P(('win', 'blk'))
- grad_codes: float32 [2048, 1920], P(('win', 'blk'))
- grad_levels: float32 [2, 1920], P(None, ('win', 'blk'))
- grad_gain: float32 [2, 1920], P(None, ('win', 'blk'))
- grad_bias: float32 [2, 1920], P(None, ('win', 'blk'))
Inputs may be any that keep to these rules, and one draw needn't show every extreme that they name: `level_ids`: each level is the level of 2 windows.
All inputs are finite; a program needn't handle non-finite values.
Results may differ from a plain program's by a relative error of at most 0.0092.
Values may be sent and summed in bfloat16 or wider, within the bound.
No kernel may reach another device: no remote copies, remote signals or barrier semaphores. Data moves between devices by JAX's collectives and lax.ppermute only.
A program may use at most 192 MiB of HBM per device.

v0:
```python
import functools

import jax
import jax.numpy as jnp
import numpy as np
from jax import lax
from jax.experimental import pallas as pl
from jax.experimental.pallas import tpu as pltpu
from jax.sharding import Mesh, PartitionSpec as P

HEAD = 480
BLOCK = 128
RATIO = 4
D = 1920
SHARDS = 128
ROWS = 16
HALF = 1024
HALVES = (slice(0, HALF), slice(HALF, 2 * HALF))
SPLITS = (1536, 1024, 896)
TOKENS = 256
CHUNK = 640
MIB = 2**20
ROW_STEP = 32
epsilon = 1e-05
bf16 = jnp.bfloat16
f32 = jnp.float32
AXES = ("yl", "co", "yh", "z", "x")
WIN = ("yl", "co")
BLK = ("yh", "z", "x")
STEP_BITS = {"x": (1, 3), "z": (4, 12), "y": (64, 80)}
CORE_BIT = 32
ORDERS = (("x", "z", "y"), ("z", "y", "x"), ("y", "x", "z"))


def exchange(value, order, step):
    masks = STEP_BITS[order[step // 2]]
    pairs = [(i, i ^ masks[(step % 2) ^ ((i >> 5) & 1)]) for i in range(SHARDS)]
    return lax.ppermute(value, AXES, pairs)


def swap_cores(value):
    return lax.ppermute(value, AXES, [(i, i ^ CORE_BIT) for i in range(SHARDS)])


def call(kernel, out_shape, vmem=32, **options):
    params = pltpu.CompilerParams(vmem_limit_bytes=vmem * MIB)
    return pl.pallas_call(kernel, out_shape=out_shape, compiler_params=params, **options)


def shape(rows, columns, dtype=bf16):
    return jax.ShapeDtypeStruct((rows, columns), dtype)


def dot(left, right):
    return jnp.dot(left, right, preferred_element_type=f32)


def rows_dot(left, right):
    return lax.dot_general(left, right, (((0,), (0,)), ((), ())), preferred_element_type=f32)


def cols_dot(left, right):
    return lax.dot_general(left, right, (((1,), (1,)), ((), ())), preferred_element_type=f32)


def hot(left, right):
    return jnp.where(left == right, 1.0, 0.0).astype(bf16)


def join_kernel(tiles, cuts, first, second, *targets):
    @pl.when(pl.program_id(0) < tiles)
    def _():
        for target, (start, stop) in zip(targets, cuts):
            target[...] = first[:, start:stop]

    @pl.when(pl.program_id(0) >= tiles)
    def _():
        for target, (start, stop) in zip(targets, cuts):
            target[...] = second[:, start:stop]


def join(first, second, cuts=None):
    rows, columns = first.shape
    cuts = cuts or ((0, columns),)
    tiles = max(rows // 128, 1)
    tile = rows // tiles
    out = call(
        functools.partial(join_kernel, tiles, cuts),
        tuple(shape(2 * rows, stop - start) for start, stop in cuts),
        grid=(2 * tiles,),
        in_specs=[
            pl.BlockSpec((tile, columns), lambda i: (jnp.minimum(i, tiles - 1), 0)),
            pl.BlockSpec((tile, columns), lambda i: (jnp.maximum(i - tiles, 0), 0)),
        ],
        out_specs=tuple(pl.BlockSpec((tile, stop - start), lambda i: (i, 0)) for start, stop in cuts),
    )(first, second)
    return out if len(cuts) > 1 else out[0]


def add_kernel(kept_low, kept_high, got_low, got_high, kept, sent):
    kept[...] = (kept_low[...].astype(f32) + got_low[...].astype(f32)).astype(bf16)
    sent[...] = (kept_high[...].astype(f32) + got_high[...].astype(f32)).astype(bf16)


def add_halves(kept, got):
    rows, columns = kept.shape[0] // 2, kept.shape[1]
    tiles = max(rows // 128, 1)
    tile = rows // tiles
    low = pl.BlockSpec((tile, columns), lambda i: (i, 0))
    high = pl.BlockSpec((tile, columns), lambda i: (i + tiles, 0))
    half = shape(rows, columns)
    return call(
        add_kernel, (half, half), grid=(tiles,), in_specs=[low, high, low, high], out_specs=(low, low)
    )(kept, kept, got, got)


def merge_kernel(*refs):
    sources, kept, sent = refs[:8], refs[8], refs[9]
    start = 0
    for one in (0, 4):
        columns = sources[one].shape[1]
        for target, low in ((kept, one), (sent, one + 1)):
            total = sources[low][...].astype(f32) + sources[low + 2][...].astype(f32)
            target[:, start : start + columns] = total.astype(bf16)
        start += columns


def merge_halves(early, early_got, late, late_got):
    rows = early.shape[0] // 2
    tiles = rows // 64
    columns = early.shape[1] + late.shape[1]
    low = lambda v: pl.BlockSpec((64, v.shape[1]), lambda i: (i, 0))
    high = lambda v: pl.BlockSpec((64, v.shape[1]), lambda i: (i + tiles, 0))
    specs = [spec(v) for v in (early, late) for spec in (low, high, low, high)]
    out = pl.BlockSpec((64, columns), lambda i: (i, 0))
    half = shape(rows, columns)
    return call(merge_kernel, (half, half), grid=(tiles,), in_specs=specs, out_specs=(out, out))(
        early, early, early_got, early_got, late, late, late_got, late_got
    )


def outer_kernel(tiles, line, extra, left, left_got, right, right_got, *refs):
    kept, sent = refs[-2:]
    rows = HALF // 2 // tiles
    columns = right.shape[1]
    step = pl.program_id(0)
    for target, base in ((kept, 0), (sent, HALF // 2)):
        start = pl.multiple_of(base + step * rows, rows)
        if line is None:
            one, two = left[:, pl.ds(start, rows)], left_got[:, pl.ds(start, rows)]
        else:
            places_here = refs[0][line : line + 1, pl.ds(start, rows)]
            one, two = hot(left[...], places_here), hot(left_got[...], places_here)
        for cut in range(0, columns, 512):
            span = slice(cut, min(cut + 512, columns))
            total = rows_dot(one, right[:, span]) + rows_dot(two, right_got[:, span])
            target[:, span] = total.astype(bf16)
        if extra == "small":
            row = lax.broadcasted_iota(jnp.int32, (rows, 64), 0) + start
            chunk = lax.broadcasted_iota(jnp.int32, (rows, 64), 1)
            target[:, columns:] = dot(hot(row, chunk * ROWS), refs[1][...]).astype(bf16)
        elif extra == "zero":
            target[:, columns:] = jnp.zeros((rows, target.shape[1] - columns), bf16)


def outer(left, left_got, right, right_got, line=None, targets=None, small=None):
    tiles = 4
    args = (left, left_got, right, right_got)
    columns = right.shape[1]
    extra = None
    if line is not None:
        args += (targets,)
    if small is not None:
        args += (small,)
        extra = "small"
        columns += 128
    elif columns % 128:
        extra = "zero"
        columns += 128 - columns % 128
    whole = lambda v: pl.BlockSpec(v.shape, lambda i: (0, 0))
    half = shape(HALF // 2, columns)
    tile = pl.BlockSpec((HALF // 2 // tiles, columns), lambda i: (i, 0))
    return call(
        functools.partial(outer_kernel, tiles, line, extra),
        (half, half),
        grid=(tiles,),
        in_specs=[whole(v) for v in args],
        out_specs=(tile, tile),
    )(*args)


def shard_tables():
    table = np.zeros((2, 8, SHARDS), np.int32)
    for core in range(2):
        for number, order in enumerate(ORDERS):
            for place in range(SHARDS):
                here = core ^ (place >> 6)
                mask = (place >> 6) * CORE_BIT
                for step in range(6):
                    if (place >> step) & 1:
                        mask ^= STEP_BITS[order[step // 2]][(step % 2) ^ here]
                table[core, number, place] = mask
    table[:, 3:5] = table[:, 1:3]
    lines = np.repeat(table, ROWS, axis=2)
    return lines, lines.transpose(0, 2, 1).copy(), table.transpose(0, 2, 1).copy()


def prepare_kernel(qkv, attn, expand, reduce, table, gain, shift, level, *outs):
    for target in outs:
        target[...] = jnp.zeros(target.shape, bf16)
    first, second, third = outs
    first[0:15, 0:1440] = qkv[...]
    first[0:15, 1440:1536] = attn[:, 384:480]
    first[0:15, 1536:1920] = attn[:, 0:384]
    second[:, 0:1024] = table[:, 0:1024]
    second[0:15, 1024:2944] = expand[...]
    third[:, 0:896] = table[:, 1024:1920]
    third[0:15, 896:2816] = reduce[...]
    for number, ref in enumerate((gain, shift, level)):
        for row in range(2):
            start = (2 * number + row) * 15
            first[15:16, start : start + 15] = ref[row : row + 1, :]


def prepare(*args):
    vmem = pl.BlockSpec(memory_space=pltpu.VMEM)
    return call(
        prepare_kernel,
        (shape(16, 1920), shape(16, 2944), shape(16, 2816)),
        in_specs=[vmem] * 8,
        out_specs=[vmem] * 3,
    )(*args)


def places_kernel(here, codes_line, lines, columns, shards, targets, target_columns, shard_column, codes):
    me, core = here[0], here[1]

    def feature_of(place, inside):
        return jnp.where(inside < 15, place * 15 + inside, -1)

    place = jnp.where(core == 0, lines[0], lines[1]) ^ me
    inside = lax.broadcasted_iota(jnp.int32, place.shape, 1) & 15
    line = lax.broadcasted_iota(jnp.int32, place.shape, 0)
    targets[...] = jnp.where(line < 3, feature_of(place, inside), place * 16 + inside)
    place = jnp.where(core == 0, columns[0], columns[1]) ^ me
    inside = lax.broadcasted_iota(jnp.int32, place.shape, 0) & 15
    target_columns[...] = feature_of(place, inside)
    shard_column[...] = jnp.where(core == 0, shards[0], shards[1]) ^ me
    row = jnp.right_shift(lax.broadcasted_iota(jnp.int32, (TOKENS, 64), 0), 2)
    column = lax.broadcasted_iota(jnp.int32, (TOKENS, 64), 1)
    spread = jnp.where(row == column, codes_line[...], 0)
    codes[...] = jnp.sum(spread, axis=1, keepdims=True)


def places(here, codes_line):
    vmem = pl.BlockSpec(memory_space=pltpu.VMEM)
    i32 = jnp.int32
    return call(
        places_kernel,
        (shape(8, 2048, i32), shape(2048, 8, i32), shape(SHARDS, 8, i32), shape(TOKENS, 1, i32)),
        in_specs=[pl.BlockSpec(memory_space=pltpu.SMEM)] + [vmem] * 4,
        out_specs=[vmem] * 4,
    )(here, codes_line, *(jnp.asarray(t) for t in shard_tables()))


class Fetch:
    def __init__(self, sources, targets, sem):
        self.copies = [
            pltpu.make_async_copy(source, target, sem.at[i])
            for i, (source, target) in enumerate(zip(sources, targets))
        ]
        self.targets = targets
        for copy in self.copies:
            copy.start()

    def __call__(self, *numbers):
        for number in numbers:
            self.copies[number].wait()
        return [self.targets[number] for number in numbers]


def fetched(arrays):
    return [pltpu.VMEM(v.shape, v.dtype) for v in arrays] + [pltpu.SemaphoreType.DMA((len(arrays),))]


def tail_lanes(value):
    source = lax.broadcasted_iota(jnp.int32, (480, 256), 0)
    target = lax.broadcasted_iota(jnp.int32, (480, 256), 1)
    return dot(value, hot(source, jnp.where(target >= 160, target + 224, -1))).astype(bf16)


def split_refs(refs, *counts):
    out, start = [], 0
    for count in counts:
        out.append(refs[start : start + count])
        start += count
    return out


def each_chunk(columns, body, width=CHUNK):
    @pl.loop(0, columns // width)
    def _(i):
        body(pl.ds(pl.multiple_of(i * width, 128), width))


def each_rows(body):
    @pl.loop(0, TOKENS // ROW_STEP)
    def _(i):
        body(pl.ds(pl.multiple_of(i * ROW_STEP, ROW_STEP), ROW_STEP))


def shuffle(value, targets, line, own, other):
    for half, target in enumerate((own, other)):

        def part(span, half=half, target=target):
            place = targets[line : line + 1, pl.ds(pl.multiple_of(span.start + half * HALF, 128), 256)]
            feature = lax.broadcasted_iota(jnp.int32, (D, 256), 0)
            target[:, span] = dot(value[...], hot(feature, place)).astype(bf16)

        each_chunk(HALF, part, 256)


def unshuffle(value, target_columns, line, out):
    def part(span):
        feature = lax.broadcasted_iota(jnp.int32, (512, CHUNK), 1) + span.start
        total = None
        for k in range(4):
            cut = slice(512 * k, 512 * k + 512)
            place = target_columns[cut, line : line + 1]
            term = dot(value[:, cut], hot(place, feature))
            total = term if total is None else total + term
        out[:, span] = total

    each_chunk(D, part)


def pieces_of(own, other):
    return [ref[:, cut] for ref in (own, other) for cut in (slice(0, 512), slice(512, 1024))]


def row_move(transposed=False):
    row = lax.broadcasted_iota(jnp.int32, (TOKENS, TOKENS), 1 if transposed else 0)
    token = lax.broadcasted_iota(jnp.int32, (TOKENS, TOKENS), 0 if transposed else 1)
    moved = jnp.right_shift(row, 3) * 4 + (row & 3) + (jnp.right_shift(row, 2) & 1) * 128
    return hot(token, moved)


def moments(value):
    average = jnp.mean(value, axis=-1, keepdims=True)
    centered = value - average
    variance = jnp.mean(centered * centered, axis=-1, keepdims=True)
    return centered, lax.rsqrt(variance + epsilon)


def norm_back(value, grad, gain, base):
    centered, scale = moments(value)
    normed = centered * scale
    scaled = grad * gain
    inner = scaled - jnp.mean(scaled, axis=-1, keepdims=True)
    inner = inner - normed * jnp.mean(scaled * normed, axis=-1, keepdims=True)
    return base + scale * inner, grad * normed


def embed_kernel(*refs):
    small, big, outs, scratch = split_refs(refs, 6, 12, 5, len(refs) - 23)
    hidden, codes, level, targets, shard_column, marks = small
    stream, own, other, packed, vectors = outs
    normed = scratch[-1]
    fetch = Fetch(big, scratch[:12], scratch[12])
    tables_a, tables_b, weights = range(0, 4), range(4, 8), range(8, 12)
    for line, numbers, start in ((3, tables_a, 0), (4, tables_b, 1024)):
        table = fetch(*numbers)
        total = None
        for k in range(4):
            term = dot(hot(codes[...], targets[line : line + 1, 512 * k : 512 * k + 512]), table[k][...])
            total = term if total is None else total + term
        stream[:, start : start + table[0].shape[1]] = total
    weight = fetch(*weights)
    chunk = lax.broadcasted_iota(jnp.int32, (SHARDS, 512), 0)
    row = lax.broadcasted_iota(jnp.int32, (SHARDS, 512), 1)
    lines = None
    for k in range(4):
        term = dot(hot(row + 512 * k, chunk * ROWS + 15), weight[k][:, :128])
        lines = term if lines is None else lines + term
    spread = rows_dot(lines.astype(bf16), hot(shard_column[:, 0:1], marks[0:1, :]))
    within = lax.broadcasted_iota(jnp.int32, (SHARDS, 1), 0)
    group = sum((within >= 15 * r).astype(jnp.int32) for r in range(1, 7))
    spread = jnp.where(within - group * 15 == marks[1:2, :], spread, 0.0).astype(bf16)
    number = lax.broadcasted_iota(jnp.int32, (8, SHARDS), 1)
    first = lax.broadcasted_iota(jnp.int32, (8, SHARDS), 0) * 15
    chosen = jnp.where((number >= first) & (number < first + 15), 1.0, 0.0).astype(bf16)
    vectors[...] = dot(chosen, spread)
    level_row = jnp.where(level[0] == 0, vectors[4:5, :], vectors[5:6, :])

    def rows(span):
        value = stream[span, :] + hidden[span, :].astype(f32) + level_row
        stream[span, :] = value
        centered, scale = moments(value)
        normed[span, :] = (centered * scale * vectors[0:1, :] + vectors[2:3, :]).astype(bf16)

    each_rows(rows)
    normed[...] = dot(row_move(), normed[...]).astype(bf16)
    shuffle(normed, targets, 0, own, other)
    packed[...] = sum(dot(p, w[:, 0:1440]) for p, w in zip(pieces_of(own, other), weight)).astype(bf16)


def embed(hidden, codes, level, targets, shard_column, marks, tables_a, tables_b, qkv):
    big = (*tables_a, *tables_b, *qkv)
    vmem = pl.BlockSpec(memory_space=pltpu.VMEM)
    return call(
        embed_kernel,
        (
            shape(TOKENS, D, f32),
            shape(TOKENS, HALF),
            shape(TOKENS, HALF),
            shape(TOKENS, 1440),
            shape(8, D, f32),
        ),
        vmem=48,
        in_specs=[vmem, vmem, pl.BlockSpec(memory_space=pltpu.SMEM), vmem, vmem, vmem]
        + [pl.BlockSpec(memory_space=pl.ANY)] * 12,
        out_specs=[vmem] * 5,
        scratch_shapes=fetched(big) + [pltpu.VMEM((TOKENS, D), bf16)],
    )(hidden, codes, level, targets, shard_column, marks, *big)


def probabilities(columns):
    query, key = columns[:, 0:480], columns[:, 480:960]
    row = lax.broadcasted_iota(jnp.int32, (TOKENS, TOKENS), 0)
    other = lax.broadcasted_iota(jnp.int32, (TOKENS, TOKENS), 1)
    mask = ((row & 3) == (other & 3)) & (jnp.right_shift(row, 2) >= jnp.right_shift(other, 2))
    scores = jnp.where(mask, cols_dot(query, key) * HEAD ** (-0.5), -1e30)
    top = jnp.max(scores, axis=-1, keepdims=True)
    total = top + jnp.log(jnp.sum(jnp.exp(scores - top), axis=-1, keepdims=True))
    return jnp.exp(scores - total)


def attend_kernel(columns, mixed):
    mixed[...] = dot(probabilities(columns).astype(bf16), columns[:, 960:1440]).astype(bf16)


def attend(columns):
    return call(attend_kernel, shape(TOKENS, 480))(columns)


def attend_back_kernel(columns, d_mixed, d_packed):
    probs = probabilities(columns)
    low = probs.astype(bf16)
    d_probs = cols_dot(d_mixed[...], columns[:, 960:1440])
    d_scores = (probs * (d_probs - jnp.sum(probs * d_probs, axis=-1, keepdims=True))).astype(bf16)
    scale = HEAD ** (-0.5)
    d_packed[:, 0:480] = (dot(d_scores, columns[:, 480:960]) * scale).astype(bf16)
    d_packed[:, 480:960] = (rows_dot(d_scores, columns[:, 0:480]) * scale).astype(bf16)
    d_packed[:, 960:1440] = rows_dot(low, d_mixed[...]).astype(bf16)


def attend_back(columns, d_mixed):
    return call(attend_back_kernel, shape(TOKENS, 1440))(columns, d_mixed)


def middle_kernel(*refs):
    small, big, outs, scratch = split_refs(refs, 6, 16, 12, len(refs) - 34)
    mixed_columns, stream, vectors, upstream, targets, target_columns = small
    block_out, d_mid, second_own, second_other, active_own, active_other = outs[:6]
    attn_own, attn_other, d_upward, mixed, d_mixed, sums = outs[6:]
    fetch = Fetch([ref.at[:, 1280:1536] for ref in big[:4]] + list(big[4:]), scratch[:16], scratch[16])
    mid, work, slope, wide, low = scratch[17:]
    rest, attn = fetch(*range(0, 4)), fetch(*range(4, 8))
    mixed[...] = dot(row_move(True), mixed_columns[...]).astype(bf16)
    end = tail_lanes(mixed[...])
    for k in range(4):
        total = cols_dot(mixed[:, 0:384], attn[k][...]) + cols_dot(end, rest[k][...])
        wide[:, 512 * k : 512 * k + 512] = total.astype(bf16)
    unshuffle(wide, target_columns, 0, work)

    def rows_first(span):
        value = stream[span, :] + work[span, :]
        mid[span, :] = value
        centered, scale = moments(value)
        low[span, :] = (centered * scale * vectors[1:2, :] + vectors[3:4, :]).astype(bf16)

    each_rows(rows_first)
    shuffle(low, targets, 1, second_own, second_other)
    expand = fetch(*range(8, 12))

    def up(span):
        parts = zip(pieces_of(second_own, second_other), expand)
        work[:, span] = sum(dot(p, w[:, span]) for p, w in parts)

    each_chunk(D, up)

    def rows_active(span):
        value = work[span, :]
        root = np.float32(np.sqrt(2 / np.pi))
        square = value * value
        bend = jnp.tanh(root * value * (1.0 + 0.044715 * square))
        low[span, :] = (0.5 * value * (1.0 + bend)).astype(bf16)
        inner = root * (1.0 + 3 * 0.044715 * square)
        slope[span, :] = 0.5 * (1.0 + bend) + 0.5 * value * (1.0 - bend * bend) * inner

    each_rows(rows_active)
    shuffle(low, targets, 2, active_own, active_other)
    reduce = fetch(*range(12, 16))

    def down(span):
        parts = zip(pieces_of(active_own, active_other), reduce)
        total = sum(dot(p, w[:, span]) for p, w in parts)
        block_out[:, span] = (mid[:, span] + total).astype(bf16)

    each_chunk(D, down)
    for k in range(4):
        wide[:, 512 * k : 512 * k + 512] = cols_dot(upstream[...], reduce[k][...]).astype(bf16)
    unshuffle(wide, target_columns, 2, work)

    def rows_upward(span):
        d_upward[span, :] = (slope[span, :] * work[span, :]).astype(bf16)

    each_rows(rows_upward)
    for k in range(4):
        wide[:, 512 * k : 512 * k + 512] = cols_dot(d_upward[...], expand[k][...]).astype(bf16)
    unshuffle(wide, target_columns, 1, work)
    sums[...] = jnp.zeros(sums.shape, f32)

    def rows_back(span):
        base = upstream[span, :].astype(f32)
        grad = work[span, :]
        value, gain_part = norm_back(mid[span, :], grad, vectors[1:2, :], base)
        d_mid[span, :] = value
        low[span, :] = value.astype(bf16)
        sums[0:1, :] += jnp.sum(gain_part, axis=0, keepdims=True)
        sums[1:2, :] += jnp.sum(grad, axis=0, keepdims=True)

    each_rows(rows_back)
    shuffle(low, targets, 0, attn_own, attn_other)
    parts = pieces_of(attn_own, attn_other)
    back = sum(dot(p, w[...]) for p, w in zip(parts, attn)).astype(bf16)
    d_mixed[:, 0:384] = dot(row_move(), back).astype(bf16)
    back = sum(dot(p, w[...]) for p, w in zip(parts, rest)).astype(bf16)
    back = dot(row_move(), back).astype(bf16)
    source = lax.broadcasted_iota(jnp.int32, (256, 128), 0)
    target = lax.broadcasted_iota(jnp.int32, (256, 128), 1)
    d_mixed[:, 384:480] = dot(back, hot(source - 160, target))[:, 0:96].astype(bf16)


def middle(mixed_columns, stream, vectors, upstream, targets, target_columns, qkv, attn, expand, reduce):
    big = (*qkv, *attn, *expand, *reduce)
    scratch = [jax.ShapeDtypeStruct((512, 256), bf16)] * 4 + list(big[4:])
    vmem = pl.BlockSpec(memory_space=pltpu.VMEM)
    half = shape(TOKENS, HALF)
    return call(
        middle_kernel,
        (shape(TOKENS, D), shape(TOKENS, D, f32))
        + (half,) * 6
        + (shape(TOKENS, D), shape(TOKENS, 480), shape(TOKENS, 480), shape(8, D, f32)),
        vmem=60,
        in_specs=[vmem] * 6 + [pl.BlockSpec(memory_space=pl.ANY)] * 16,
        out_specs=[vmem] * 12,
        scratch_shapes=fetched(scratch)
        + [pltpu.VMEM((TOKENS, D), f32)] * 3
        + [pltpu.VMEM((TOKENS, 2 * HALF), bf16), pltpu.VMEM((TOKENS, D), bf16)],
    )(mixed_columns, stream, vectors, upstream, targets, target_columns, *big)


def last_kernel(*refs):
    small, big, outs, scratch = split_refs(refs, 9, 4, 4, len(refs) - 17)
    d_packed, stream, d_mid, vectors, sums, level, target_columns, shard_column, marks = small
    d_stream, low_a, low_b, spread = outs
    fetch = Fetch(big, scratch[:4], scratch[4])
    work, wide, totals = scratch[5:]
    weight = fetch(*range(4))
    for k in range(4):
        wide[:, 512 * k : 512 * k + 512] = cols_dot(d_packed[...], weight[k][:, 0:1440]).astype(bf16)
    wide[...] = dot(row_move(True), wide[...]).astype(bf16)
    unshuffle(wide, target_columns, 0, work)
    totals[...] = jnp.zeros(totals.shape, f32)

    def rows(span):
        grad = work[span, :]
        value, gain_part = norm_back(stream[span, :], grad, vectors[0:1, :], d_mid[span, :])
        d_stream[span, :] = value
        low_a[span, :] = value[:, 0:1024].astype(bf16)
        low_b[span, :] = value[:, 1024:1920].astype(bf16)
        totals[0:1, :] += jnp.sum(gain_part, axis=0, keepdims=True)
        totals[2:3, :] += jnp.sum(grad, axis=0, keepdims=True)
        totals[6:7, :] += jnp.sum(value, axis=0, keepdims=True)

    each_rows(rows)
    totals[1:2, :] = sums[0:1, :]
    totals[3:4, :] = sums[1:2, :]
    totals[4:5, :] = jnp.where(level[0] == 0, totals[6:7, :], 0.0)
    totals[5:6, :] = jnp.where(level[0] == 1, totals[6:7, :], 0.0)
    number = lax.broadcasted_iota(jnp.int32, (SHARDS, 8), 0)
    first = lax.broadcasted_iota(jnp.int32, (SHARDS, 8), 1) * 15
    chosen = jnp.where((number >= first) & (number < first + 15) & (number < 90), 1.0, 0.0)
    repeated = dot(chosen.astype(bf16), totals[...].astype(bf16))
    within = lax.broadcasted_iota(jnp.int32, (SHARDS, 1), 0)
    group = sum((within >= 15 * r).astype(jnp.int32) for r in range(1, 7))
    repeated = jnp.where(within - group * 15 == marks[1:2, :], repeated, 0.0).astype(bf16)
    spread[...] = cols_dot(hot(shard_column[:, 2:3], marks[0:1, :]), repeated).astype(bf16)


def last(d_packed, stream, d_mid, vectors, sums, level, target_columns, shard_column, marks, qkv):
    vmem = pl.BlockSpec(memory_space=pltpu.VMEM)
    return call(
        last_kernel,
        (shape(TOKENS, D, f32), shape(TOKENS, 1024), shape(TOKENS, 896), shape(SHARDS, 128)),
        vmem=40,
        in_specs=[vmem] * 5
        + [pl.BlockSpec(memory_space=pltpu.SMEM)]
        + [vmem] * 3
        + [pl.BlockSpec(memory_space=pl.ANY)] * 4,
        out_specs=[vmem] * 4,
        scratch_shapes=fetched(qkv)
        + [
            pltpu.VMEM((TOKENS, D), f32),
            pltpu.VMEM((TOKENS, 2 * HALF), bf16),
            pltpu.VMEM((8, D), f32),
        ],
    )(d_packed, stream, d_mid, vectors, sums, level, target_columns, shard_column, marks, *qkv)


def finish_kernel(kept0, got0, kept1, got1, kept2, got2, *outs):
    grad_qkv, grad_attn, grad_expand, grad_reduce, table, levels, gains, shifts = outs

    def total(kept, got, start, stop):
        return kept[:, start:stop].astype(f32) + got[:, start:stop].astype(f32)

    grad_attn[...] = total(kept0, got0, 0, 480)[:15]
    grad_qkv[...] = total(kept0, got0, 512, 1952)[:15]
    grad_expand[...] = total(kept1, got1, 0, 1920)[:15]
    table[:, 0:1024] = total(kept1, got1, 1920, 2944)
    grad_reduce[...] = total(kept2, got2, 0, 1920)[:15]
    table[:, 1024:1920] = total(kept2, got2, 1920, 2816)
    line = total(kept2, got2, 2816, 2944)[0:1]
    for target, first in ((gains, 0), (shifts, 2), (levels, 4)):
        for row in range(2):
            start = (first + row) * 15
            target[row : row + 1, :] = line[:, start : start + 15]


def finish(*pairs):
    vmem = pl.BlockSpec(memory_space=pltpu.VMEM)
    return call(
        finish_kernel,
        tuple(
            shape(*s, f32)
            for s in ((15, 1440), (15, 480), (15, D), (15, D), (16, D), (2, 15), (2, 15), (2, 15))
        ),
        in_specs=[vmem] * 6,
        out_specs=[vmem] * 8,
    )(*pairs)


def body(
    hidden_in,
    cond_codes,
    level_ids,
    qkv_weight,
    attn_out_weight,
    mlp_in_weight,
    mlp_out_weight,
    code_table,
    level_table,
    norm_gain,
    norm_bias,
    grad_out,
):
    yl, co, yh, z, x = (lax.axis_index(name) for name in AXES)
    me = yl * 64 + co * 32 + yh * 16 + z * 4 + x
    targets, target_columns, shard_column, codes = places(jnp.stack((me, co)), cond_codes)
    shards = prepare(
        qkv_weight,
        attn_out_weight.T,
        mlp_in_weight,
        mlp_out_weight,
        code_table,
        norm_gain,
        norm_bias,
        level_table,
    )
    feature = np.arange(D, dtype=np.int32)
    marks = jnp.asarray(np.stack((feature // 15, feature % 15)))

    small = [join(buf, exchange(buf, order, 0)) for buf, order in zip(shards, ORDERS)]
    small, (targets, target_columns, shard_column, codes) = lax.optimization_barrier(
        (small, (targets, target_columns, shard_column, codes))
    )
    for step in (1, 2):
        small = [join(buf, exchange(buf, order, step)) for buf, order in zip(small, ORDERS)]
    small = [
        join(buf, exchange(buf, order, 3), ((0, split), (split, buf.shape[1])))
        for buf, order, split in zip(small, ORDERS, SPLITS)
    ]
    halves = [join(buf, exchange(buf, order, 4)) for (buf, _), order in zip(small, ORDERS)]
    rests = [exchange(half, order, 5) for half, order in zip(halves, ORDERS)]
    pieces = [(h, r, swap_cores(h), swap_cores(r)) for h, r in zip(halves, rests)]
    pieces, small = lax.optimization_barrier((pieces, [buf for _, buf in small]))
    qkv, table_a, table_b = pieces
    halves = [join(buf, exchange(buf, order, 4)) for buf, order in zip(small, ORDERS)]

    stream, first_own, first_other, packed, vectors = embed(
        hidden_in[0], codes, level_ids, targets, shard_column, marks, table_a, table_b, qkv
    )
    packed, halves = lax.optimization_barrier((packed, halves))
    rests = [exchange(half, order, 5) for half, order in zip(halves, ORDERS)]
    attn, expand, reduce = [(h, r, swap_cores(h), swap_cores(r)) for h, r in zip(halves, rests)]

    def over_blocks(value):
        return lax.all_to_all(value, BLK, split_axis=0, concat_axis=0, tiled=True)

    columns = over_blocks(packed)
    mixed = over_blocks(attend(columns))
    upstream = grad_out[0]
    (
        block_out,
        d_mid,
        second_own,
        second_other,
        active_own,
        active_other,
        attn_own,
        attn_other,
        d_upward,
        mixed,
        d_mixed,
        sums,
    ) = middle(mixed, stream, vectors, upstream, targets, target_columns, qkv, attn, expand, reduce)
    d_mixed = over_blocks(d_mixed)
    early = [
        outer(own, swap_cores(other), right, swap_cores(right))
        for own, other, right in (
            (attn_own, attn_other, mixed),
            (second_own, second_other, d_upward),
            (active_own, active_other, upstream),
        )
    ]
    early_got = [exchange(sent, order, 5) for (_, sent), order in zip(early, ORDERS)]
    first_got = swap_cores(first_other)
    codes_got = swap_cores(codes)

    d_packed = attend_back(columns, d_mixed)
    d_packed, early_got = lax.optimization_barrier((d_packed, early_got))
    d_packed = over_blocks(d_packed)
    early = [add_halves(kept, got) for (kept, _), got in zip(early, early_got)]
    d_packed, early = lax.optimization_barrier((d_packed, early))
    early_got = [exchange(sent, order, 4) for (_, sent), order in zip(early, ORDERS)]
    qkv_grad = outer(first_own, first_got, d_packed, swap_cores(d_packed))
    d_packed, qkv_grad = lax.optimization_barrier((d_packed, qkv_grad))

    d_stream, low_a, low_b, small = last(
        d_packed, stream, d_mid, vectors, sums, level_ids, target_columns, shard_column, marks, qkv
    )
    small = small[:64] + swap_cores(small[64:])
    grad_a = outer(codes, codes_got, low_a, swap_cores(low_a), 3, targets)
    grad_b = outer(codes, codes_got, low_b, swap_cores(low_b), 4, targets, small)
    pairs = []
    for (kept, sent), (before, _), before_got, order in zip(
        (qkv_grad, grad_a, grad_b), early, early_got, ORDERS
    ):
        kept, sent = add_halves(kept, exchange(sent, order, 5))
        kept, sent = merge_halves(before, before_got, kept, exchange(sent, order, 4))
        for step in (3, 2, 1):
            kept, sent = add_halves(kept, exchange(sent, order, step))
        pairs += [kept, exchange(sent, order, 0)]
    grad_qkv, grad_attn, grad_expand, grad_reduce, grad_table, levels, gains, shifts = finish(*pairs)
    return (
        block_out[None],
        d_stream[None],
        grad_qkv,
        grad_attn.T,
        grad_expand,
        grad_reduce,
        grad_table,
        levels,
        gains,
        shifts,
    )


def solution(mesh):
    fine = Mesh(mesh.devices.reshape(2, 2, 2, 4, 4), AXES)
    return jax.shard_map(
        body,
        mesh=fine,
        in_specs=(
            P(WIN, BLK, None),
            P(WIN, BLK),
            P(WIN),
            P(AXES, None),
            P(None, AXES),
            P(AXES, None),
            P(AXES, None),
            P(AXES, None),
            P(None, AXES),
            P(None, AXES),
            P(None, AXES),
            P(WIN, BLK, None),
        ),
        out_specs=(
            P(WIN, BLK, None),
            P(WIN, BLK, None),
            P(AXES, None),
            P(None, AXES),
            P(AXES, None),
            P(AXES, None),
            P(AXES, None),
            P(None, AXES),
            P(None, AXES),
            P(None, AXES),
        ),
        check_vma=False,
    )
```

profile of v0, /device:TPU:0, one launch (start us, length us, event | category | flops | bytes accessed | tf_op | source)
XLA Modules:
  0.0 453.7 jit_solution(13272880737374081187)
XLA Ops:
  23.8 6.1 %collective-permute-done.4.second = bf16[64,1920]{1,0:T(8,128)(2,1)S(1)} collective-permute-done((bf16[64,1920]{1,0:T(8,128)(2,1)S(1)}, bf16[64,1920]{1,0:T(8,128)(2,1)S(1)}, u32[]{:S(2)}, u32[]{:S(2)}) %collective-permute-start.4) | collective-permute-done | bytes 245792 | tf_op jit(solution)/shard_map/ppermute | solution.py:38
  33.3 6.8 %collective-permute-done.5.second = bf16[128,1920]{1,0:T(8,128)(2,1)S(1)} collective-permute-done((bf16[128,1920]{1,0:T(8,128)(2,1)S(1)}, bf16[128,1920]{1,0:T(8,128)(2,1)S(1)}, u32[]{:S(2)}, u32[]{:S(2)}) %collective-permute-start.5) | collective-permute-done | bytes 491552 | tf_op jit(solution)/shard_map/ppermute | solution.py:38
  45.8 5.7 %collective-permute-done.17.second = bf16[32,2816]{1,0:T(8,128)(2,1)S(1)} collective-permute-done((bf16[32,2816]{1,0:T(8,128)(2,1)S(1)}, bf16[32,2816]{1,0:T(8,128)(2,1)S(1)}, u32[]{:S(2)}, u32[]{:S(2)}) %collective-permute-start.17) | collective-permute-done | bytes 180256 | tf_op jit(solution)/shard_map/ppermute | solution.py:38
  51.6 6.7 %collective-permute-done.11.second = bf16[64,2944]{1,0:T(8,128)(2,1)S(1)} collective-permute-done((bf16[64,2944]{1,0:T(8,128)(2,1)S(1)}, bf16[64,2944]{1,0:T(8,128)(2,1)S(1)}, u32[]{:S(2)}, u32[]{:S(2)}) %collective-permute-start.11) | collective-permute-done | bytes 376864 | tf_op jit(solution)/shard_map/ppermute | solution.py:38
  63.8 5.3 %collective-permute-start.7 = (bf16[512,1536]{1,0:T(8,128)(2,1)S(1)}, bf16[512,1536]{1,0:T(8,128)(2,1)S(1)}, u32[]{:S(2)}, u32[]{:S(2)}) collective-permute-start(bf16[512,1536]{1,0:T(8,128)(2,1)S(1)} %shard_map.239.refs_14_.refs_6_.refs_9_), channel_id=1, source_target_pairs={{0,80},{1,81},{2,82},{3,83},{4,84},{5,85},{6,86},{7,87},{8,88},{9,... | collective-permute-start | bytes 4718600 | tf_op jit(solution)/shard_map/ppermute | solution.py:38
  83.3 6.1 %collective-permute-done.20.second = bf16[256,896]{1,0:T(8,128)(2,1)S(1)} collective-permute-done((bf16[256,896]{1,0:T(8,128)(2,1)S(1)}, bf16[256,896]{1,0:T(8,128)(2,1)S(1)}, u32[]{:S(2)}, u32[]{:S(2)}) %collective-permute-start.20) | collective-permute-done | bytes 458784 | tf_op jit(solution)/shard_map/ppermute | solution.py:38
  89.5 7.8 %collective-permute-start.21 = (bf16[512,896]{1,0:T(8,128)(2,1)S(1)}, bf16[512,896]{1,0:T(8,128)(2,1)S(1)}, u32[]{:S(2)}, u32[]{:S(2)}) collective-permute-start(bf16[512,896]{1,0:T(8,128)(2,1)S(1)} %shard_map.247.refs_10_), channel_id=1, source_target_pairs={{0,12},{1,13},{2,14},{3,15},{4,8},{5,9},{6,10},{7,11},{8,4},{9,5},... | collective-permute-start | bytes 2752520 | tf_op jit(solution)/shard_map/ppermute | solution.py:38
  97.9 10.8 %collective-permute-done.21.refs_11_ = bf16[512,896]{1,0:T(8,128)(2,1)S(1)} collective-permute-done((bf16[512,896]{1,0:T(8,128)(2,1)S(1)}, bf16[512,896]{1,0:T(8,128)(2,1)S(1)}, u32[]{:S(2)}, u32[]{:S(2)}) %collective-permute-start.21) | collective-permute-done | bytes 917536 | tf_op jit(solution)/shard_map/ppermute | solution.py:38
  116.5 14.7 %shard_map.248 = (f32[256,1920]{1,0:T(8,128)}, bf16[256,1024]{1,0:T(8,128)(2,1)S(1)}, bf16[256,1024]{1,0:T(8,128)(2,1)S(1)}, bf16[256,1440]{1,0:T(8,128)(2,1)S(1)}, f32[8,1920]{1,0:T(8,128)S(1)}) custom-call(bf16[256,1920]{1,0:T(8,128)(2,1)} %bitcast.28, s32[256,1]{1,0:T(8,128)S(1)} %get-tuple-element.147.refs_1_.left, s32[1]{0:T(128)S(6)} %copy.28.refs_2_.refs_5_, ...), custom_call_target="tpu_custom_call" | custom-call | tf_op jit(solution)/shard_map/pallas_call | solution.py:410
  149.6 18.5 %collective-permute-done.30.refs_15_ = bf16[512,1920]{1,0:T(8,128)(2,1)} collective-permute-done((bf16[512,1920]{1,0:T(8,128)(2,1)}, bf16[512,1920]{1,0:T(8,128)(2,1)}, u32[]{:S(2)}, u32[]{:S(2)}) %collective-permute-start.30) | collective-permute-done | bytes 1966112 | tf_op jit(solution)/shard_map/ppermute | solution.py:38
  168.1 5.1 %collective-permute-start.32 = (bf16[512,1920]{1,0:T(8,128)(2,1)}, bf16[512,1920]{1,0:T(8,128)(2,1)}, u32[]{:S(2)}, u32[]{:S(2)}) collective-permute-start(bf16[512,1920]{1,0:T(8,128)(2,1)} %collective-permute-done.30.refs_15_), channel_id=1, source_target_pairs={{0,32},{1,33},{2,34},{3,35},{4,36},{5,37},{6,38},{7,39},{8,40},{9,... | collective-permute-start | bytes 5898248 | tf_op jit(solution)/shard_map/ppermute | solution.py:42
  174.1 6.5 %all-to-all-start = ((bf16[32,8,1440]{2,1,0:T(8,128)(2,1)}), bf16[32,8,1440]{2,1,0:T(8,128)(2,1)S(1)}, u32[]{:S(2)}, u32[]{:S(2)}) async-start(bf16[32,8,1440]{2,1,0:T(8,128)(2,1)} %bitcast.25), calls=%async_computation | async-start | bytes 1572864 | tf_op jit(solution)/shard_map/all_to_all | solution.py:709
  184.9 11.7 %all-to-all-done = bf16[32,8,1440]{2,1,0:T(8,128)(2,1)S(1)} async-done(((bf16[32,8,1440]{2,1,0:T(8,128)(2,1)}), bf16[32,8,1440]{2,1,0:T(8,128)(2,1)S(1)}, u32[]{:S(2)}, u32[]{:S(2)}) %all-to-all-start) | async-done | bytes 737312 | tf_op jit(solution)/shard_map/all_to_all | solution.py:709
  203.0 10.1 %all-to-all-done.1 = bf16[32,8,480]{2,1,0:T(8,128)(2,1)S(1)} async-done(((bf16[32,8,480]{2,1,0:T(8,128)(2,1)}), bf16[32,8,480]{2,1,0:T(8,128)(2,1)S(1)}, u32[]{:S(2)}, u32[]{:S(2)}) %all-to-all-start.1) | async-done | bytes 245792 | tf_op jit(solution)/shard_map/all_to_all | solution.py:709
  213.8 45.3 %shard_map.253 = (bf16[256,1920]{1,0:T(8,128)(2,1)}, f32[256,1920]{1,0:T(8,128)}, bf16[256,1024]{1,0:T(8,128)(2,1)}, bf16[256,1024]{1,0:T(8,128)(2,1)}, bf16[256...) custom-call(bf16[256,480]{1,0:T(8,128)(2,1)} %bitcast.27, ...), custom_call_target="tpu_custom_call" | custom-call | tf_op jit(solution)/shard_map/pallas_call | solution.py:550
  280.5 23.4 %all_to_all.45 = bf16[32,8,480]{2,1,0:T(8,128)(2,1)S(1)} all-to-all(bf16[32,8,480]{2,1,0:T(8,128)(2,1)S(1)} %bitcast.29), channel_id=1, replica_groups=mesh['yl'=2,'co'=2,'yh'=2,'z'=4,'x'=4] {'yh','z','x'}, dimensions={0} | all-to-all | bytes 491520 | tf_op jit(solution)/shard_map/all_to_all | solution.py:709
  309.4 6.7 %all-to-all-start.3 = ((bf16[32,8,1440]{2,1,0:T(8,128)(2,1)}), bf16[32,8,1440]{2,1,0:T(8,128)(2,1)S(1)}, u32[]{:S(2)}, u32[]{:S(2)}) async-start(bf16[32,8,1440]{2,1,0:T(8,128)(2,1)} %bitcast.12), calls=%async_computation.3 | async-start | bytes 1572864 | tf_op jit(solution)/shard_map/all_to_all | solution.py:709
  323.8 6.6 %all-to-all-done.3 = bf16[32,8,1440]{2,1,0:T(8,128)(2,1)S(1)} async-done(((bf16[32,8,1440]{2,1,0:T(8,128)(2,1)}), bf16[32,8,1440]{2,1,0:T(8,128)(2,1)S(1)}, u32[]{:S(2)}, u32[]{:S(2)}) %all-to-all-start.3) | async-done | bytes 737312 | tf_op jit(solution)/shard_map/all_to_all | solution.py:709
  350.5 10.4 %shard_map.262 = (f32[256,1920]{1,0:T(8,128)}, bf16[256,1024]{1,0:T(8,128)(2,1)S(1)}, bf16[256,896]{1,0:T(8,128)(2,1)S(1)}, bf16[128,128]{1,0:T(8,128)(2,1)S(1)}) custom-call(bf16[256,1440]{1,0:T(8,128)(2,1)S(1)} %bitcast.18, f32[256,1920]{1,0:T(8,128)S(1)} %copy-done.11, f32[256,1920]{1,0:T(8,128)S(1)} %copy-done.31, f32[8,1920]{1,0:T(8,128)S(1)} %copy-done.50, ...), custom_call_target="tpu_custom_call" | custom-call | tf_op jit(solution)/shard_map/pallas_call | solution.py:604
  372.5 20.0 %collective-permute-done.66.got_low.got_high = bf16[512,1024]{1,0:T(8,128)(2,1)S(1)} collective-permute-done((bf16[512,1024]{1,0:T(8,128)(2,1)S(1)}, bf16[512,1024]{1,0:T(8,128)(2,1)S(1)}, u32[]{:S(2)}, u32[]{:S(2)}) %collective-permute-start.66) | collective-permute-done | bytes 1048608 | tf_op jit(solution)/shard_map/ppermute | solution.py:38
  392.9 5.3 %collective-permute-done.57.got_low.got_high = bf16[512,1024]{1,0:T(8,128)(2,1)S(1)} collective-permute-done((bf16[512,1024]{1,0:T(8,128)(2,1)S(1)}, bf16[512,1024]{1,0:T(8,128)(2,1)S(1)}, u32[]{:S(2)}, u32[]{:S(2)}) %collective-permute-start.57) | collective-permute-done | bytes 1048608 | tf_op jit(solution)/shard_map/ppermute | solution.py:38
  403.9 9.0 %collective-permute-done.58.refs_6_.refs_7_ = bf16[256,1024]{1,0:T(8,128)(2,1)S(1)} collective-permute-done((bf16[256,1024]{1,0:T(8,128)(2,1)S(1)}, bf16[256,1024]{1,0:T(8,128)(2,1)S(1)}, u32[]{:S(2)}, u32[]{:S(2)}) %collective-permute-start.58) | collective-permute-done | bytes 524320 | tf_op jit(solution)/shard_map/ppermute | solution.py:38
  416.0 6.4 %collective-permute-done.47.refs_2_.refs_3_ = bf16[256,512]{1,0:T(8,128)(2,1)S(1)} collective-permute-done((bf16[256,512]{1,0:T(8,128)(2,1)S(1)}, bf16[256,512]{1,0:T(8,128)(2,1)S(1)}, u32[]{:S(2)}, u32[]{:S(2)}) %collective-permute-start.47) | collective-permute-done | bytes 262176 | tf_op jit(solution)/shard_map/ppermute | solution.py:38
  428.9 6.2 %collective-permute-done.50.got_low.got_high = bf16[128,2048]{1,0:T(8,128)(2,1)S(1)} collective-permute-done((bf16[128,2048]{1,0:T(8,128)(2,1)S(1)}, bf16[128,2048]{1,0:T(8,128)(2,1)S(1)}, u32[]{:S(2)}, u32[]{:S(2)}) %collective-permute-start.50) | collective-permute-done | bytes 524320 | tf_op jit(solution)/shard_map/ppermute | solution.py:38
  (338 shorter events, 190.0 us)
Async XLA Ops:
  40.2 23.4 %collective-permute-start.6 = (bf16[256,1536]{1,0:T(8,128)(2,1)S(1)}, bf16[256,1536]{1,0:T(8,128)(2,1)S(1)}, u32[]{:S(2)}, u32[]{:S(2)}) collective-permute-start(bf16[256,1536]{1,0:T(8,128)(2,1)S(1)} %get-tuple-element.151.first), channel_id=1, source_target_pairs={{0,64},{1,65},{2,66},{3,67},{4,68},{5,69},{6,70},{7,71},{8,72},{9,... | collective-permute-start | bytes 2359304 | tf_op jit(solution)/shard_map/ppermute | solution.py:38
  63.8 34.0 %collective-permute-start.7 = (bf16[512,1536]{1,0:T(8,128)(2,1)S(1)}, bf16[512,1536]{1,0:T(8,128)(2,1)S(1)}, u32[]{:S(2)}, u32[]{:S(2)}) collective-permute-start(bf16[512,1536]{1,0:T(8,128)(2,1)S(1)} %shard_map.239.refs_14_.refs_6_.refs_9_), channel_id=1, source_target_pairs={{0,80},{1,81},{2,82},{3,83},{4,84},{5,85},{6,86},{7,87},{8,88},{9,... | collective-permute-start | bytes 4718600 | tf_op jit(solution)/shard_map/ppermute | solution.py:38
  80.9 27.8 %collective-permute-start.14 = (bf16[512,1024]{1,0:T(8,128)(2,1)S(1)}, bf16[512,1024]{1,0:T(8,128)(2,1)S(1)}, u32[]{:S(2)}, u32[]{:S(2)}) collective-permute-start(bf16[512,1024]{1,0:T(8,128)(2,1)S(1)} %shard_map.243.refs_6_), channel_id=1, source_target_pairs={{0,3},{1,2},{2,1},{3,0},{4,7},{5,6},{6,5},{7,4},{8,11},{9,10},{10,... | collective-permute-start | bytes 3145736 | tf_op jit(solution)/shard_map/ppermute | solution.py:38
  114.2 19.2 %collective-permute-start.26 = (bf16[256,1920]{1,0:T(8,128)(2,1)S(1)}, bf16[256,1920]{1,0:T(8,128)(2,1)S(1)}, u32[]{:S(2)}, u32[]{:S(2)}) collective-permute-start(bf16[256,1920]{1,0:T(8,128)(2,1)S(1)} %get-tuple-element.174.first), channel_id=1, source_target_pairs={{0,4},{1,5},{2,6},{3,7},{4,0},{5,1},{6,2},{7,3},{8,12},{9,13},{10,... | collective-permute-start | bytes 2949128 | tf_op jit(solution)/shard_map/ppermute | solution.py:38
  115.3 21.8 %collective-permute-start.25 = (bf16[256,1920]{1,0:T(8,128)(2,1)S(1)}, bf16[256,1920]{1,0:T(8,128)(2,1)}, u32[]{:S(2)}, u32[]{:S(2)}) collective-permute-start(bf16[256,1920]{1,0:T(8,128)(2,1)S(1)} %get-tuple-element.173.first), channel_id=1, source_target_pairs={{0,1},{1,0},{2,3},{3,2},{4,5},{5,4},{6,7},{7,6},{8,9},{9,8},{10,11... | collective-permute-start | bytes 2949128 | tf_op jit(solution)/shard_map/ppermute | solution.py:38
  141.4 26.7 %collective-permute-start.30 = (bf16[512,1920]{1,0:T(8,128)(2,1)}, bf16[512,1920]{1,0:T(8,128)(2,1)}, u32[]{:S(2)}, u32[]{:S(2)}) collective-permute-start(bf16[512,1920]{1,0:T(8,128)(2,1)} %shard_map.250.refs_14_), channel_id=1, source_target_pairs={{0,3},{1,2},{2,1},{3,0},{4,7},{5,6},{6,5},{7,4},{8,11},{9,10},{10,... | collective-permute-start | bytes 5898248 | tf_op jit(solution)/shard_map/ppermute | solution.py:38
  145.1 28.1 %collective-permute-start.33 = (bf16[512,1920]{1,0:T(8,128)(2,1)S(1)}, bf16[512,1920]{1,0:T(8,128)(2,1)}, u32[]{:S(2)}, u32[]{:S(2)}) collective-permute-start(bf16[512,1920]{1,0:T(8,128)(2,1)S(1)} %shard_map.251.refs_18_), channel_id=1, source_target_pairs={{0,12},{1,13},{2,14},{3,15},{4,8},{5,9},{6,10},{7,11},{8,4},{9,5},... | collective-permute-start | bytes 5898248 | tf_op jit(solution)/shard_map/ppermute | solution.py:38
  148.4 64.7 %collective-permute-start.31 = (bf16[512,1920]{1,0:T(8,128)(2,1)}, bf16[512,1920]{1,0:T(8,128)(2,1)}, u32[]{:S(2)}, u32[]{:S(2)}) collective-permute-start(bf16[512,1920]{1,0:T(8,128)(2,1)} %shard_map.250.refs_14_), channel_id=1, source_target_pairs={{0,32},{1,33},{2,34},{3,35},{4,36},{5,37},{6,38},{7,39},{8,40},{9,... | collective-permute-start | bytes 5898248 | tf_op jit(solution)/shard_map/ppermute | solution.py:42
  149.5 63.6 %collective-permute-start.34 = (bf16[512,1920]{1,0:T(8,128)(2,1)S(1)}, bf16[512,1920]{1,0:T(8,128)(2,1)}, u32[]{:S(2)}, u32[]{:S(2)}) collective-permute-start(bf16[512,1920]{1,0:T(8,128)(2,1)S(1)} %shard_map.251.refs_18_), channel_id=1, source_target_pairs={{0,32},{1,33},{2,34},{3,35},{4,36},{5,37},{6,38},{7,39},{8,40},{9,... | collective-permute-start | bytes 5898248 | tf_op jit(solution)/shard_map/ppermute | solution.py:42
  168.1 45.0 %collective-permute-start.32 = (bf16[512,1920]{1,0:T(8,128)(2,1)}, bf16[512,1920]{1,0:T(8,128)(2,1)}, u32[]{:S(2)}, u32[]{:S(2)}) collective-permute-start(bf16[512,1920]{1,0:T(8,128)(2,1)} %collective-permute-done.30.refs_15_), channel_id=1, source_target_pairs={{0,32},{1,33},{2,34},{3,35},{4,36},{5,37},{6,38},{7,39},{8,40},{9,... | collective-permute-start | bytes 5898248 | tf_op jit(solution)/shard_map/ppermute | solution.py:42
  173.2 39.9 %collective-permute-start.35 = (bf16[512,1920]{1,0:T(8,128)(2,1)}, bf16[512,1920]{1,0:T(8,128)(2,1)}, u32[]{:S(2)}, u32[]{:S(2)}) collective-permute-start(bf16[512,1920]{1,0:T(8,128)(2,1)} %collective-permute-done.33.refs_19_), channel_id=1, source_target_pairs={{0,32},{1,33},{2,34},{3,35},{4,36},{5,37},{6,38},{7,39},{8,40},{9,... | collective-permute-start | bytes 5898248 | tf_op jit(solution)/shard_map/ppermute | solution.py:42
  174.1 22.5 %all-to-all-start = ((bf16[32,8,1440]{2,1,0:T(8,128)(2,1)}), bf16[32,8,1440]{2,1,0:T(8,128)(2,1)S(1)}, u32[]{:S(2)}, u32[]{:S(2)}) async-start(bf16[32,8,1440]{2,1,0:T(8,128)(2,1)} %bitcast.25), calls=%async_computation | async-start | bytes 1572864 | tf_op jit(solution)/shard_map/all_to_all | solution.py:709
  202.7 57.3 %collective-permute-start.43 = (bf16[256,1920]{1,0:T(8,128)(2,1)}, bf16[256,1920]{1,0:T(8,128)(2,1)}, u32[]{:S(2)}, u32[]{:S(2)}) collective-permute-start(bf16[256,1920]{1,0:T(8,128)(2,1)} %bitcast.21), channel_id=1, source_target_pairs={{0,32},{1,33},{2,34},{3,35},{4,36},{5,37},{6,38},{7,39},{8,40},{9,... | collective-permute-start | bytes 2949128 | tf_op jit(solution)/shard_map/ppermute | solution.py:42
  269.5 37.1 %collective-permute-start.44 = (bf16[512,1920]{1,0:T(8,128)(2,1)S(1)}, bf16[512,1920]{1,0:T(8,128)(2,1)S(1)}, u32[]{:S(2)}, u32[]{:S(2)}) collective-permute-start(bf16[512,1920]{1,0:T(8,128)(2,1)S(1)} %get-tuple-element.194), channel_id=1, source_target_pairs={{0,12},{1,13},{2,14},{3,15},{4,8},{5,9},{6,10},{7,11},{8,4},{9,5},... | collective-permute-start | bytes 5898248 | tf_op jit(solution)/shard_map/ppermute | solution.py:38
  274.0 34.0 %collective-permute-start.41 = (bf16[512,1920]{1,0:T(8,128)(2,1)S(1)}, bf16[512,1920]{1,0:T(8,128)(2,1)S(1)}, u32[]{:S(2)}, u32[]{:S(2)}) collective-permute-start(bf16[512,1920]{1,0:T(8,128)(2,1)S(1)} %get-tuple-element.191), channel_id=1, source_target_pairs={{0,3},{1,2},{2,1},{3,0},{4,7},{5,6},{6,5},{7,4},{8,11},{9,10},{10,... | collective-permute-start | bytes 5898248 | tf_op jit(solution)/shard_map/ppermute | solution.py:38
  279.6 26.3 %collective-permute-start.38 = (bf16[512,512]{1,0:T(8,128)(2,1)S(1)}, bf16[512,512]{1,0:T(8,128)(2,1)S(1)}, u32[]{:S(2)}, u32[]{:S(2)}) collective-permute-start(bf16[512,512]{1,0:T(8,128)(2,1)S(1)} %get-tuple-element.187), channel_id=1, source_target_pairs={{0,80},{1,81},{2,82},{3,83},{4,84},{5,85},{6,86},{7,87},{8,88},{9,... | collective-permute-start | bytes 1572872 | tf_op jit(solution)/shard_map/ppermute | solution.py:38
  309.4 21.0 %all-to-all-start.3 = ((bf16[32,8,1440]{2,1,0:T(8,128)(2,1)}), bf16[32,8,1440]{2,1,0:T(8,128)(2,1)S(1)}, u32[]{:S(2)}, u32[]{:S(2)}) async-start(bf16[32,8,1440]{2,1,0:T(8,128)(2,1)} %bitcast.12), calls=%async_computation.3 | async-start | bytes 1572864 | tf_op jit(solution)/shard_map/all_to_all | solution.py:709
  361.5 37.0 %collective-permute-start.48 = (bf16[512,1536]{1,0:T(8,128)(2,1)S(1)}, bf16[512,1536]{1,0:T(8,128)(2,1)S(1)}, u32[]{:S(2)}, u32[]{:S(2)}) collective-permute-start(bf16[512,1536]{1,0:T(8,128)(2,1)S(1)} %get-tuple-element.220), channel_id=1, source_target_pairs={{0,80},{1,81},{2,82},{3,83},{4,84},{5,85},{6,86},{7,87},{8,88},{9,... | collective-permute-start | bytes 4718600 | tf_op jit(solution)/shard_map/ppermute | solution.py:38
  367.4 25.1 %collective-permute-start.66 = (bf16[512,1024]{1,0:T(8,128)(2,1)S(1)}, bf16[512,1024]{1,0:T(8,128)(2,1)S(1)}, u32[]{:S(2)}, u32[]{:S(2)}) collective-permute-start(bf16[512,1024]{1,0:T(8,128)(2,1)S(1)} %get-tuple-element.251), channel_id=1, source_target_pairs={{0,12},{1,13},{2,14},{3,15},{4,8},{5,9},{6,10},{7,11},{8,4},{9,5},... | collective-permute-start | bytes 3145736 | tf_op jit(solution)/shard_map/ppermute | solution.py:38
  370.9 27.3 %collective-permute-start.57 = (bf16[512,1024]{1,0:T(8,128)(2,1)S(1)}, bf16[512,1024]{1,0:T(8,128)(2,1)S(1)}, u32[]{:S(2)}, u32[]{:S(2)}) collective-permute-start(bf16[512,1024]{1,0:T(8,128)(2,1)S(1)} %get-tuple-element.235), channel_id=1, source_target_pairs={{0,3},{1,2},{2,1},{3,0},{4,7},{5,6},{6,5},{7,4},{8,11},{9,10},{10,... | collective-permute-start | bytes 3145736 | tf_op jit(solution)/shard_map/ppermute | solution.py:38
  372.4 27.5 %collective-permute-start.63 = (bf16[256,1920]{1,0:T(8,128)(2,1)S(1)}, bf16[256,1920]{1,0:T(8,128)(2,1)S(1)}, u32[]{:S(2)}, u32[]{:S(2)}) collective-permute-start(bf16[256,1920]{1,0:T(8,128)(2,1)S(1)} %copy-done.67), channel_id=1, source_target_pairs={{0,4},{1,5},{2,6},{3,7},{4,0},{5,1},{6,2},{7,3},{8,12},{9,13},{10,... | collective-permute-start | bytes 2949128 | tf_op jit(solution)/shard_map/ppermute | solution.py:38
  372.4 31.5 %collective-permute-start.54 = (bf16[256,1920]{1,0:T(8,128)(2,1)S(1)}, bf16[256,1920]{1,0:T(8,128)(2,1)S(1)}, u32[]{:S(2)}, u32[]{:S(2)}) collective-permute-start(bf16[256,1920]{1,0:T(8,128)(2,1)S(1)} %copy-done.65), channel_id=1, source_target_pairs={{0,1},{1,0},{2,3},{3,2},{4,5},{5,4},{6,7},{7,6},{8,9},{9,8},{10,11... | collective-permute-start | bytes 2949128 | tf_op jit(solution)/shard_map/ppermute | solution.py:38
  399.0 23.5 %collective-permute-start.49 = (bf16[256,1536]{1,0:T(8,128)(2,1)S(1)}, bf16[256,1536]{1,0:T(8,128)(2,1)S(1)}, u32[]{:S(2)}, u32[]{:S(2)}) collective-permute-start(bf16[256,1536]{1,0:T(8,128)(2,1)S(1)} %get-tuple-element.222), channel_id=1, source_target_pairs={{0,64},{1,65},{2,66},{3,67},{4,68},{5,69},{6,70},{7,71},{8,72},{9,... | collective-permute-start | bytes 2359304 | tf_op jit(solution)/shard_map/ppermute | solution.py:38
  402.4 21.9 %collective-permute-start.68 = (bf16[128,2944]{1,0:T(8,128)(2,1)S(1)}, bf16[128,2944]{1,0:T(8,128)(2,1)S(1)}, u32[]{:S(2)}, u32[]{:S(2)}) collective-permute-start(bf16[128,2944]{1,0:T(8,128)(2,1)S(1)} %get-tuple-element.255), channel_id=1, source_target_pairs={{0,3},{1,2},{2,1},{3,0},{4,7},{5,6},{6,5},{7,4},{8,11},{9,10},{10,... | collective-permute-start | bytes 2261000 | tf_op jit(solution)/shard_map/ppermute | solution.py:38
  (129 other events, 1087.9 us)
where the time goes:
time: 462 us; the launch traced here: 454 us
  waiting for transfers between devices  179 us (39%)
  Pallas kernels  103 us (22%)
  starting transfers between devices  102 us (22%)
  local copies, waits for them, and re-layouts  43.3 us (9%)
  blocking collectives  23.4 us (5%)
    ppermute x48, waiting for transfers between devices, exchange(): return lax.ppermute(value, AXES, pairs)  137 us
    ppermute x48, starting transfers between devices, exchange(): return lax.ppermute(value, AXES, pairs)  72.8 us
    pallas_call x1, Pallas kernels, middle(): call(middle_kernel, (shape(TOKENS, D), shape(TOKENS, D, f32)) + (half,) *...  45.3 us
    unnamed x156, local copies, waits for them, and re-layouts  39.8 us
    all_to_all x3, waiting for transfers between devices, over_blocks(): return lax.all_to_all(value, BLK, split_axis=0, concat_axis=0, tiled=True)  28.3 us
    all_to_all x1, blocking collectives, over_blocks(): return lax.all_to_all(value, BLK, split_axis=0, concat_axis=0, tiled=True)  23.4 us
    all_to_all x3, starting transfers between devices, over_blocks(): return lax.all_to_all(value, BLK, split_axis=0, concat_axis=0, tiled=True)  17.7 us
    pallas_call x6, Pallas kernels, outer(): call(functools.partial(outer_kernel, tiles, line, extra), (half, half), g...  17.2 us
  transfers between devices with their start and end apart: 75, of which 35 were waited for; matrix products, arithmetic and copies ran while one was open for 1% of the time, Pallas kernels for 18%

commit v1 on v0

--- a/solution.py
+++ b/solution.py
@@ -42,9 +42,28 @@
     return lax.ppermute(value, AXES, [(i, i ^ CORE_BIT) for i in range(SHARDS)])
 
 
-def call(kernel, out_shape, vmem=32, **options):
+def call(kernel, out_shape, vmem=32, flops=0, **options):
     params = pltpu.CompilerParams(vmem_limit_bytes=vmem * MIB)
-    return pl.pallas_call(kernel, out_shape=out_shape, compiler_params=params, **options)
+
+    def run(*args):
+        outs = out_shape if isinstance(out_shape, tuple) else (out_shape,)
+        size = sum(v.size * v.dtype.itemsize for v in args + outs)
+        cost = pl.CostEstimate(flops=int(flops), bytes_accessed=size, transcendentals=0)
+        return pl.pallas_call(
+            kernel, out_shape=out_shape, compiler_params=params, cost_estimate=cost, **options
+        )(*args)
+
+    return run
+
+
+def whole(v):
+    return pl.BlockSpec(
+        v.shape, lambda i: (0,) * len(v.shape), pipeline_mode=pl.Buffered(buffer_count=1)
+    )
+
+
+def outs_whole(shapes):
+    return tuple(pl.BlockSpec(v.shape, lambda i: (0, 0)) for v in shapes)
 
 
 def shape(rows, columns, dtype=bf16):
@@ -67,76 +86,83 @@
     return jnp.where(left == right, 1.0, 0.0).astype(bf16)
 
 
-def join_kernel(tiles, cuts, first, second, *targets):
-    @pl.when(pl.program_id(0) < tiles)
-    def _():
-        for target, (start, stop) in zip(targets, cuts):
-            target[...] = first[:, start:stop]
-
-    @pl.when(pl.program_id(0) >= tiles)
-    def _():
-        for target, (start, stop) in zip(targets, cuts):
-            target[...] = second[:, start:stop]
-
-
-def join(first, second, cuts=None):
-    rows, columns = first.shape
-    cuts = cuts or ((0, columns),)
+def join_kernel(tiles, cuts, *refs):
+    count = len(cuts)
+    sources, targets = refs[: 2 * count], list(refs[2 * count :])
+    step = pl.program_id(0)
+    for i, spans in enumerate(cuts):
+        mine, targets = targets[: len(spans)], targets[len(spans) :]
+        for source, here in ((sources[2 * i], step < tiles), (sources[2 * i + 1], step >= tiles)):
+
+            @pl.when(here)
+            def _(source=source, mine=mine, spans=spans):
+                for target, (start, stop) in zip(mine, spans):
+                    target[...] = source[:, start:stop]
+
+
+def join(firsts, seconds, cuts=None):
+    rows = firsts[0].shape[0]
+    cuts = cuts or [((0, v.shape[1]),) for v in firsts]
     tiles = max(rows // 128, 1)
     tile = rows // tiles
+    specs, args = [], []
+    for first, second in zip(firsts, seconds):
+        columns = first.shape[1]
+        specs += [
+            pl.BlockSpec((tile, columns), lambda i: (jnp.minimum(i, tiles - 1), 0)),
+            pl.BlockSpec((tile, columns), lambda i: (jnp.maximum(i - tiles, 0), 0)),
+        ]
+        args += [first, second]
+    widths = [stop - start for spans in cuts for start, stop in spans]
     out = call(
         functools.partial(join_kernel, tiles, cuts),
-        tuple(shape(2 * rows, stop - start) for start, stop in cuts),
+        tuple(shape(2 * rows, width) for width in widths),
         grid=(2 * tiles,),
-        in_specs=[
-            pl.BlockSpec((tile, columns), lambda i: (jnp.minimum(i, tiles - 1), 0)),
-            pl.BlockSpec((tile, columns), lambda i: (jnp.maximum(i - tiles, 0), 0)),
-        ],
-        out_specs=tuple(pl.BlockSpec((tile, stop - start), lambda i: (i, 0)) for start, stop in cuts),
-    )(first, second)
-    return out if len(cuts) > 1 else out[0]
-
-
-def add_kernel(kept_low, kept_high, got_low, got_high, kept, sent):
-    kept[...] = (kept_low[...].astype(f32) + got_low[...].astype(f32)).astype(bf16)
-    sent[...] = (kept_high[...].astype(f32) + got_high[...].astype(f32)).astype(bf16)
-
-
-def add_halves(kept, got):
-    rows, columns = kept.shape[0] // 2, kept.shape[1]
+        in_specs=specs,
+        out_specs=tuple(pl.BlockSpec((tile, width), lambda i: (i, 0)) for width in widths),
+    )(*args)
+    out = list(out)
+    return [[out.pop(0) for _ in spans] for spans in cuts]
+
+
+def add_kernel(counts, *refs):
+    arrays = sum(counts)
+    sources, targets = refs[: 4 * arrays], refs[4 * arrays :]
+    number = 0
+    for i, count in enumerate(counts):
+        start = 0
+        for _ in range(count):
+            kept_low, kept_high, got_low, got_high = sources[4 * number : 4 * number + 4]
+            span = slice(start, start + kept_low.shape[1])
+            targets[2 * i][:, span] = (kept_low[...].astype(f32) + got_low[...].astype(f32)).astype(bf16)
+            targets[2 * i + 1][:, span] = (
+                kept_high[...].astype(f32) + got_high[...].astype(f32)
+            ).astype(bf16)
+            start, number = span.stop, number + 1
+
+
+def add_halves(groups):
+    rows = groups[0][0][0].shape[0] // 2
     tiles = max(rows // 128, 1)
     tile = rows // tiles
-    low = pl.BlockSpec((tile, columns), lambda i: (i, 0))
-    high = pl.BlockSpec((tile, columns), lambda i: (i + tiles, 0))
-    half = shape(rows, columns)
-    return call(
-        add_kernel, (half, half), grid=(tiles,), in_specs=[low, high, low, high], out_specs=(low, low)
-    )(kept, kept, got, got)
-
-
-def merge_kernel(*refs):
-    sources, kept, sent = refs[:8], refs[8], refs[9]
-    start = 0
-    for one in (0, 4):
-        columns = sources[one].shape[1]
-        for target, low in ((kept, one), (sent, one + 1)):
-            total = sources[low][...].astype(f32) + sources[low + 2][...].astype(f32)
-            target[:, start : start + columns] = total.astype(bf16)
-        start += columns
-
-
-def merge_halves(early, early_got, late, late_got):
-    rows = early.shape[0] // 2
-    tiles = rows // 64
-    columns = early.shape[1] + late.shape[1]
-    low = lambda v: pl.BlockSpec((64, v.shape[1]), lambda i: (i, 0))
-    high = lambda v: pl.BlockSpec((64, v.shape[1]), lambda i: (i + tiles, 0))
-    specs = [spec(v) for v in (early, late) for spec in (low, high, low, high)]
-    out = pl.BlockSpec((64, columns), lambda i: (i, 0))
-    half = shape(rows, columns)
-    return call(merge_kernel, (half, half), grid=(tiles,), in_specs=specs, out_specs=(out, out))(
-        early, early, early_got, early_got, late, late, late_got, late_got
-    )
+    specs, args, widths = [], [], []
+    for group in groups:
+        for kept, got in group:
+            columns = kept.shape[1]
+            low = pl.BlockSpec((tile, columns), lambda i: (i, 0))
+            high = pl.BlockSpec((tile, columns), lambda i: (i + tiles, 0))
+            specs += [low, high, low, high]
+            args += [kept, kept, got, got]
+        widths.append(sum(kept.shape[1] for kept, _ in group))
+    out = call(
+        functools.partial(add_kernel, [len(group) for group in groups]),
+        tuple(shape(rows, width) for width in widths for _ in range(2)),
+        vmem=48,
+        grid=(tiles,),
+        in_specs=specs,
+        out_specs=tuple(pl.BlockSpec((tile, width), lambda i: (i, 0)) for width in widths for _ in range(2)),
+    )(*args)
+    return [(out[2 * i], out[2 * i + 1]) for i in range(len(groups))]
 
 
 def outer_kernel(tiles, line, extra, left, left_got, right, right_got, *refs):
@@ -177,12 +203,12 @@
     elif columns % 128:
         extra = "zero"
         columns += 128 - columns % 128
-    whole = lambda v: pl.BlockSpec(v.shape, lambda i: (0, 0))
     half = shape(HALF // 2, columns)
     tile = pl.BlockSpec((HALF // 2 // tiles, columns), lambda i: (i, 0))
     return call(
         functools.partial(outer_kernel, tiles, line, extra),
         (half, half),
+        flops=2 * 512 * HALF * columns,
         grid=(tiles,),
         in_specs=[whole(v) for v in args],
         out_specs=(tile, tile),
@@ -223,12 +249,13 @@
 
 
 def prepare(*args):
-    vmem = pl.BlockSpec(memory_space=pltpu.VMEM)
+    outs = (shape(16, 1920), shape(16, 2944), shape(16, 2816))
     return call(
         prepare_kernel,
-        (shape(16, 1920), shape(16, 2944), shape(16, 2816)),
-        in_specs=[vmem] * 8,
-        out_specs=[vmem] * 3,
+        outs,
+        grid=(1,),
+        in_specs=[whole(v) for v in args],
+        out_specs=outs_whole(outs),
     )(*args)
 
 
@@ -253,14 +280,16 @@
 
 
 def places(here, codes_line):
-    vmem = pl.BlockSpec(memory_space=pltpu.VMEM)
     i32 = jnp.int32
+    args = (codes_line, *(jnp.asarray(t) for t in shard_tables()))
+    outs = (shape(8, 2048, i32), shape(2048, 8, i32), shape(SHARDS, 8, i32), shape(TOKENS, 1, i32))
     return call(
         places_kernel,
-        (shape(8, 2048, i32), shape(2048, 8, i32), shape(SHARDS, 8, i32), shape(TOKENS, 1, i32)),
-        in_specs=[pl.BlockSpec(memory_space=pltpu.SMEM)] + [vmem] * 4,
-        out_specs=[vmem] * 4,
-    )(here, codes_line, *(jnp.asarray(t) for t in shard_tables()))
+        outs,
+        grid=(1,),
+        in_specs=[pl.BlockSpec(memory_space=pltpu.SMEM)] + [whole(v) for v in args],
+        out_specs=outs_whole(outs),
+    )(here, *args)
 
 
 class Fetch:
@@ -363,7 +392,7 @@
 
 def embed_kernel(*refs):
     small, big, outs, scratch = split_refs(refs, 6, 12, 5, len(refs) - 23)
-    hidden, codes, level, targets, shard_column, marks = small
+    level, hidden, codes, targets, shard_column, marks = small
     stream, own, other, packed, vectors = outs
     normed = scratch[-1]
     fetch = Fetch(big, scratch[:12], scratch[12])
@@ -404,24 +433,28 @@
     packed[...] = sum(dot(p, w[:, 0:1440]) for p, w in zip(pieces_of(own, other), weight)).astype(bf16)
 
 
-def embed(hidden, codes, level, targets, shard_column, marks, tables_a, tables_b, qkv):
+def embed(level, hidden, codes, targets, shard_column, marks, tables_a, tables_b, qkv):
     big = (*tables_a, *tables_b, *qkv)
-    vmem = pl.BlockSpec(memory_space=pltpu.VMEM)
+    args = (hidden, codes, targets, shard_column, marks)
+    outs = (
+        shape(TOKENS, D, f32),
+        shape(TOKENS, HALF),
+        shape(TOKENS, HALF),
+        shape(TOKENS, 1440),
+        shape(8, D, f32),
+    )
     return call(
         embed_kernel,
-        (
-            shape(TOKENS, D, f32),
-            shape(TOKENS, HALF),
-            shape(TOKENS, HALF),
-            shape(TOKENS, 1440),
-            shape(8, D, f32),
-        ),
-        vmem=48,
-        in_specs=[vmem, vmem, pl.BlockSpec(memory_space=pltpu.SMEM), vmem, vmem, vmem]
+        outs,
+        vmem=52,
+        flops=8e9,
+        grid=(1,),
+        in_specs=[pl.BlockSpec(memory_space=pltpu.SMEM)]
+        + [whole(v) for v in args]
         + [pl.BlockSpec(memory_space=pl.ANY)] * 12,
-        out_specs=[vmem] * 5,
+        out_specs=outs_whole(outs),
         scratch_shapes=fetched(big) + [pltpu.VMEM((TOKENS, D), bf16)],
-    )(hidden, codes, level, targets, shard_column, marks, *big)
+    )(level, *args, *big)
 
 
 def probabilities(columns):
@@ -440,7 +473,10 @@
 
 
 def attend(columns):
-    return call(attend_kernel, shape(TOKENS, 480))(columns)
+    out = shape(TOKENS, 480)
+    return call(
+        attend_kernel, out, grid=(1,), in_specs=[whole(columns)], out_specs=whole(out)
+    )(columns)
 
 
 def attend_back_kernel(columns, d_mixed, d_packed):
@@ -452,10 +488,18 @@
     d_packed[:, 0:480] = (dot(d_scores, columns[:, 480:960]) * scale).astype(bf16)
     d_packed[:, 480:960] = (rows_dot(d_scores, columns[:, 0:480]) * scale).astype(bf16)
     d_packed[:, 960:1440] = rows_dot(low, d_mixed[...]).astype(bf16)
+    d_packed[:, 1440:1536] = jnp.zeros((TOKENS, 96), bf16)
 
 
 def attend_back(columns, d_mixed):
-    return call(attend_back_kernel, shape(TOKENS, 1440))(columns, d_mixed)
+    out = shape(TOKENS, 1536)
+    return call(
+        attend_back_kernel,
+        out,
+        grid=(1,),
+        in_specs=[whole(columns), whole(d_mixed)],
+        out_specs=whole(out),
+    )(columns, d_mixed)
 
 
 def middle_kernel(*refs):
@@ -466,8 +510,9 @@
     fetch = Fetch([ref.at[:, 1280:1536] for ref in big[:4]] + list(big[4:]), scratch[:16], scratch[16])
     mid, work, slope, wide, low = scratch[17:]
     rest, attn = fetch(*range(0, 4)), fetch(*range(4, 8))
-    mixed[...] = dot(row_move(True), mixed_columns[...]).astype(bf16)
-    end = tail_lanes(mixed[...])
+    mixed[:, 480:512] = jnp.zeros((TOKENS, 32), bf16)
+    mixed[:, 0:480] = dot(row_move(True), mixed_columns[...]).astype(bf16)
+    end = tail_lanes(mixed[:, 0:480])
     for k in range(4):
         total = cols_dot(mixed[:, 0:384], attn[k][...]) + cols_dot(end, rest[k][...])
         wide[:, 512 * k : 512 * k + 512] = total.astype(bf16)
@@ -545,31 +590,36 @@
 def middle(mixed_columns, stream, vectors, upstream, targets, target_columns, qkv, attn, expand, reduce):
     big = (*qkv, *attn, *expand, *reduce)
     scratch = [jax.ShapeDtypeStruct((512, 256), bf16)] * 4 + list(big[4:])
-    vmem = pl.BlockSpec(memory_space=pltpu.VMEM)
+    args = (mixed_columns, stream, vectors, upstream, targets, target_columns)
     half = shape(TOKENS, HALF)
+    outs = (
+        (shape(TOKENS, D), shape(TOKENS, D, f32))
+        + (half,) * 6
+        + (shape(TOKENS, D), shape(TOKENS, 512), shape(TOKENS, 480), shape(8, D, f32))
+    )
     return call(
         middle_kernel,
-        (shape(TOKENS, D), shape(TOKENS, D, f32))
-        + (half,) * 6
-        + (shape(TOKENS, D), shape(TOKENS, 480), shape(TOKENS, 480), shape(8, D, f32)),
+        outs,
         vmem=60,
-        in_specs=[vmem] * 6 + [pl.BlockSpec(memory_space=pl.ANY)] * 16,
-        out_specs=[vmem] * 12,
+        flops=25e9,
+        grid=(1,),
+        in_specs=[whole(v) for v in args] + [pl.BlockSpec(memory_space=pl.ANY)] * 16,
+        out_specs=tuple(whole(v) for v in outs),
         scratch_shapes=fetched(scratch)
         + [pltpu.VMEM((TOKENS, D), f32)] * 3
         + [pltpu.VMEM((TOKENS, 2 * HALF), bf16), pltpu.VMEM((TOKENS, D), bf16)],
-    )(mixed_columns, stream, vectors, upstream, targets, target_columns, *big)
+    )(*args, *big)
 
 
 def last_kernel(*refs):
     small, big, outs, scratch = split_refs(refs, 9, 4, 4, len(refs) - 17)
-    d_packed, stream, d_mid, vectors, sums, level, target_columns, shard_column, marks = small
+    level, d_packed, stream, d_mid, vectors, sums, target_columns, shard_column, marks = small
     d_stream, low_a, low_b, spread = outs
     fetch = Fetch(big, scratch[:4], scratch[4])
     work, wide, totals = scratch[5:]
     weight = fetch(*range(4))
     for k in range(4):
-        wide[:, 512 * k : 512 * k + 512] = cols_dot(d_packed[...], weight[k][:, 0:1440]).astype(bf16)
+        wide[:, 512 * k : 512 * k + 512] = cols_dot(d_packed[:, 0:1440], weight[k][:, 0:1440]).astype(bf16)
     wide[...] = dot(row_move(True), wide[...]).astype(bf16)
     unshuffle(wide, target_columns, 0, work)
     totals[...] = jnp.zeros(totals.shape, f32)
@@ -599,24 +649,26 @@
     spread[...] = cols_dot(hot(shard_column[:, 2:3], marks[0:1, :]), repeated).astype(bf16)
 
 
-def last(d_packed, stream, d_mid, vectors, sums, level, target_columns, shard_column, marks, qkv):
-    vmem = pl.BlockSpec(memory_space=pltpu.VMEM)
+def last(level, d_packed, stream, d_mid, vectors, sums, target_columns, shard_column, marks, qkv):
+    args = (d_packed, stream, d_mid, vectors, sums, target_columns, shard_column, marks)
+    outs = (shape(TOKENS, D, f32), shape(TOKENS, 1024), shape(TOKENS, 896), shape(SHARDS, 128))
     return call(
         last_kernel,
-        (shape(TOKENS, D, f32), shape(TOKENS, 1024), shape(TOKENS, 896), shape(SHARDS, 128)),
-        vmem=40,
-        in_specs=[vmem] * 5
-        + [pl.BlockSpec(memory_space=pltpu.SMEM)]
-        + [vmem] * 3
+        outs,
+        vmem=48,
+        flops=6e9,
+        grid=(1,),
+        in_specs=[pl.BlockSpec(memory_space=pltpu.SMEM)]
+        + [whole(v) for v in args]
         + [pl.BlockSpec(memory_space=pl.ANY)] * 4,
-        out_specs=[vmem] * 4,
+        out_specs=tuple(whole(v) for v in outs),
         scratch_shapes=fetched(qkv)
         + [
             pltpu.VMEM((TOKENS, D), f32),
             pltpu.VMEM((TOKENS, 2 * HALF), bf16),
             pltpu.VMEM((8, D), f32),
         ],
-    )(d_packed, stream, d_mid, vectors, sums, level, target_columns, shard_column, marks, *qkv)
+    )(level, *args, *qkv)
 
 
 def finish_kernel(kept0, got0, kept1, got1, kept2, got2, *outs):
@@ -639,15 +691,16 @@
 
 
 def finish(*pairs):
-    vmem = pl.BlockSpec(memory_space=pltpu.VMEM)
+    outs = tuple(
+        shape(*s, f32)
+        for s in ((15, 1440), (15, 480), (15, D), (15, D), (16, D), (2, 15), (2, 15), (2, 15))
+    )
     return call(
         finish_kernel,
-        tuple(
-            shape(*s, f32)
-            for s in ((15, 1440), (15, 480), (15, D), (15, D), (16, D), (2, 15), (2, 15), (2, 15))
-        ),
-        in_specs=[vmem] * 6,
-        out_specs=[vmem] * 8,
+        outs,
+        grid=(1,),
+        in_specs=[whole(v) for v in pairs],
+        out_specs=outs_whole(outs),
     )(*pairs)
 
 
@@ -681,35 +734,43 @@
     feature = np.arange(D, dtype=np.int32)
     marks = jnp.asarray(np.stack((feature // 15, feature % 15)))
 
-    small = [join(buf, exchange(buf, order, 0)) for buf, order in zip(shards, ORDERS)]
+    def exchanged(values, step):
+        return [exchange(v, order, step) for v, order in zip(values, ORDERS)]
+
+    def singles(lists):
+        return [v for (v,) in lists]
+
+    small = singles(join(shards, exchanged(shards, 0)))
     small, (targets, target_columns, shard_column, codes) = lax.optimization_barrier(
         (small, (targets, target_columns, shard_column, codes))
     )
     for step in (1, 2):
-        small = [join(buf, exchange(buf, order, step)) for buf, order in zip(small, ORDERS)]
-    small = [
-        join(buf, exchange(buf, order, 3), ((0, split), (split, buf.shape[1])))
-        for buf, order, split in zip(small, ORDERS, SPLITS)
-    ]
-    halves = [join(buf, exchange(buf, order, 4)) for (buf, _), order in zip(small, ORDERS)]
-    rests = [exchange(half, order, 5) for half, order in zip(halves, ORDERS)]
-    pieces = [(h, r, swap_cores(h), swap_cores(r)) for h, r in zip(halves, rests)]
-    pieces, small = lax.optimization_barrier((pieces, [buf for _, buf in small]))
+        small = singles(join(small, exchanged(small, step)))
+    cuts = [((0, split), (split, v.shape[1])) for v, split in zip(small, SPLITS)]
+    small = join(small, exchanged(small, 3), cuts)
+    first, second = [v for v, _ in small], [v for _, v in small]
+    first = singles(join(first, exchanged(first, 4)))
+    first, second = lax.optimization_barrier((first, second))
+    rests = exchanged(first, 5)
+    second_got = exchanged(second, 4)
+    pieces = [(h, r, swap_cores(h), swap_cores(r)) for h, r in zip(first, rests)]
+    second = singles(join(second, second_got))
+    pieces, second = lax.optimization_barrier((pieces, second))
     qkv, table_a, table_b = pieces
-    halves = [join(buf, exchange(buf, order, 4)) for buf, order in zip(small, ORDERS)]
+    rests = exchanged(second, 5)
 
     stream, first_own, first_other, packed, vectors = embed(
-        hidden_in[0], codes, level_ids, targets, shard_column, marks, table_a, table_b, qkv
-    )
-    packed, halves = lax.optimization_barrier((packed, halves))
-    rests = [exchange(half, order, 5) for half, order in zip(halves, ORDERS)]
-    attn, expand, reduce = [(h, r, swap_cores(h), swap_cores(r)) for h, r in zip(halves, rests)]
+        level_ids, hidden_in[0], codes, targets, shard_column, marks, table_a, table_b, qkv
+    )
 
     def over_blocks(value):
         return lax.all_to_all(value, BLK, split_axis=0, concat_axis=0, tiled=True)
 
     columns = over_blocks(packed)
-    mixed = over_blocks(attend(columns))
+    mixed = attend(columns)
+    mixed, rests = lax.optimization_barrier((mixed, rests))
+    mixed = over_blocks(mixed)
+    attn, expand, reduce = [(h, r, swap_cores(h), swap_cores(r)) for h, r in zip(second, rests)]
     upstream = grad_out[0]
     (
         block_out,
@@ -734,34 +795,38 @@
             (active_own, active_other, upstream),
         )
     ]
-    early_got = [exchange(sent, order, 5) for (_, sent), order in zip(early, ORDERS)]
+    early_got = exchanged([sent for _, sent in early], 5)
     first_got = swap_cores(first_other)
     codes_got = swap_cores(codes)
 
-    d_packed = attend_back(columns, d_mixed)
-    d_packed, early_got = lax.optimization_barrier((d_packed, early_got))
-    d_packed = over_blocks(d_packed)
-    early = [add_halves(kept, got) for (kept, _), got in zip(early, early_got)]
+    d_packed = over_blocks(attend_back(columns, d_mixed))
+    early = add_halves([[(kept, got)] for (kept, _), got in zip(early, early_got)])
     d_packed, early = lax.optimization_barrier((d_packed, early))
-    early_got = [exchange(sent, order, 4) for (_, sent), order in zip(early, ORDERS)]
+    early_got = exchanged([sent for _, sent in early], 4)
     qkv_grad = outer(first_own, first_got, d_packed, swap_cores(d_packed))
     d_packed, qkv_grad = lax.optimization_barrier((d_packed, qkv_grad))
 
     d_stream, low_a, low_b, small = last(
-        d_packed, stream, d_mid, vectors, sums, level_ids, target_columns, shard_column, marks, qkv
+        level_ids, d_packed, stream, d_mid, vectors, sums, target_columns, shard_column, marks, qkv
     )
     small = small[:64] + swap_cores(small[64:])
     grad_a = outer(codes, codes_got, low_a, swap_cores(low_a), 3, targets)
     grad_b = outer(codes, codes_got, low_b, swap_cores(low_b), 4, targets, small)
-    pairs = []
-    for (kept, sent), (before, _), before_got, order in zip(
-        (qkv_grad, grad_a, grad_b), early, early_got, ORDERS
-    ):
-        kept, sent = add_halves(kept, exchange(sent, order, 5))
-        kept, sent = merge_halves(before, before_got, kept, exchange(sent, order, 4))
-        for step in (3, 2, 1):
-            kept, sent = add_halves(kept, exchange(sent, order, step))
-        pairs += [kept, exchange(sent, order, 0)]
+    late = [qkv_grad, grad_a, grad_b]
+    late_got = exchanged([sent for _, sent in late], 5)
+    late = add_halves([[(kept, got)] for (kept, _), got in zip(late, late_got)])
+    late_got = exchanged([sent for _, sent in late], 4)
+    sums = add_halves(
+        [
+            [(before, before_got), (kept, got)]
+            for (before, _), before_got, (kept, _), got in zip(early, early_got, late, late_got)
+        ]
+    )
+    for step in (3, 2, 1):
+        got = exchanged([sent for _, sent in sums], step)
+        sums = add_halves([[(kept, v)] for (kept, _), v in zip(sums, got)])
+    got = exchanged([sent for _, sent in sums], 0)
+    pairs = [v for (kept, _), mine in zip(sums, got) for v in (kept, mine)]
     grad_qkv, grad_attn, grad_expand, grad_reduce, grad_table, levels, gains, shifts = finish(*pairs)
     return (
         block_out[None],

time: 462 us -> 431 us (0.933)
  blocking collectives: 23.4 us -> 0 us
  local copies, waits for them, and re-layouts: 43.3 us -> 30 us
  Pallas kernels: 103 us -> 113 us
  starting transfers between devices: 102 us -> 95.2 us
    all_to_all x1 -> x0, blocking collectives: 23.4 us -> none  [over_blocks(): return lax.all_to_all(value, BLK, split_axis=0, concat_axis=0, tiled=True)]
    all_to_all x3 -> x4, waiting for transfers between devices: 28.3 us -> 45 us  [over_blocks(): return lax.all_to_all(value, BLK, split_axis=0, concat_axis=0, tiled=True)]
    ppermute x48, waiting for transfers between devices: 137 us -> 122 us  [exchange(): return lax.ppermute(value, AXES, pairs)]
    unnamed x156 -> x130, local copies, waits for them, and re-layouts: 39.8 us -> 30 us
    pallas_call x50 -> x26, Pallas kernels: 103 us -> 113 us  [run(): pl.pallas_call(kernel, out_shape=out_shape, compiler_params=params, cost_...]
    ppermute x48, starting transfers between devices: 72.8 us -> 63.5 us  [exchange(): return lax.ppermute(value, AXES, pairs)]
    all_to_all x3 -> x4, starting transfers between devices: 17.7 us -> 23.2 us  [over_blocks(): return lax.all_to_all(value, BLK, split_axis=0, concat_axis=0, tiled=True)]
  transfers between devices with their start and end apart: 75 -> 76, of which waited for: 35 -> 33; matrix products, arithmetic and copies ran while one was open for 1% -> 0% of each run, Pallas kernels for 18% -> 21%
where the time goes in v1:
time: 431 us; the launch traced here: 422 us
  waiting for transfers between devices  182 us (42%)
  Pallas kernels  113 us (26%)
  starting transfers between devices  95.2 us (22%)
  local copies, waits for them, and re-layouts  30 us (7%)
    ppermute x48, waiting for transfers between devices, exchange(): return lax.ppermute(value, AXES, pairs)  122 us
    pallas_call x26, Pallas kernels, run(): pl.pallas_call(kernel, out_shape=out_shape, compiler_params=params, cost_...  113 us
    ppermute x48, starting transfers between devices, exchange(): return lax.ppermute(value, AXES, pairs)  63.5 us
    all_to_all x4, waiting for transfers between devices, over_blocks(): return lax.all_to_all(value, BLK, split_axis=0, concat_axis=0, tiled=True)  45 us
    unnamed x130, local copies, waits for them, and re-layouts  30 us
    all_to_all x4, starting transfers between devices, over_blocks(): return lax.all_to_all(value, BLK, split_axis=0, concat_axis=0, tiled=True)  23.2 us
    ppermute x24, waiting for transfers between devices, swap_cores(): return lax.ppermute(value, AXES, [(i, i ^ CORE_BIT) for i in range(SHARDS)])  15.2 us
  transfers between devices with their start and end apart: 76, of which 33 were waited for; matrix products, arithmetic and copies ran while one was open for 0% of the time, Pallas kernels for 21%

profile of v1, /device:TPU:0, one launch (start us, length us, event | category | flops | bytes accessed | tf_op | source)
XLA Modules:
  0.0 422.5 jit_solution(10485720705418004712)
XLA Ops:
  30.1 5.2 %collective-permute-done.6.refs_1_ = bf16[64,1920]{1,0:T(8,128)(2,1)S(1)} collective-permute-done((bf16[64,1920]{1,0:T(8,128)(2,1)S(1)}, bf16[64,1920]{1,0:T(8,128)(2,1)S(1)}, u32[]{:S(2)}, u32[]{:S(2)}) %collective-permute-start.6) | collective-permute-done | bytes 245792 | tf_op jit(solution)/shard_map/ppermute | solution.py:38
  40.7 8.9 %collective-permute-done.9.refs_1_ = bf16[128,1920]{1,0:T(8,128)(2,1)S(1)} collective-permute-done((bf16[128,1920]{1,0:T(8,128)(2,1)S(1)}, bf16[128,1920]{1,0:T(8,128)(2,1)S(1)}, u32[]{:S(2)}, u32[]{:S(2)}) %collective-permute-start.9) | collective-permute-done | bytes 491552 | tf_op jit(solution)/shard_map/ppermute | solution.py:38
  52.6 7.8 %collective-permute-done.14.refs_5_ = bf16[256,896]{1,0:T(8,128)(2,1)S(1)} collective-permute-done((bf16[256,896]{1,0:T(8,128)(2,1)S(1)}, bf16[256,896]{1,0:T(8,128)(2,1)S(1)}, u32[]{:S(2)}, u32[]{:S(2)}) %collective-permute-start.14) | collective-permute-done | bytes 458784 | tf_op jit(solution)/shard_map/ppermute | solution.py:38
  69.1 5.0 %collective-permute-start.18 = (bf16[512,1024]{1,0:T(8,128)(2,1)S(1)}, bf16[512,1024]{1,0:T(8,128)(2,1)S(1)}, u32[]{:S(2)}, u32[]{:S(2)}) collective-permute-start(bf16[512,1024]{1,0:T(8,128)(2,1)S(1)} %get-tuple-element.197.refs_6_), channel_id=1, source_target_pairs={{0,3},{1,2},{2,1},{3,0},{4,7},{5,6},{6,5},{7,4},{8,11},{9,10},{10,... | collective-permute-start | bytes 3145736 | tf_op jit(solution)/shard_map/ppermute | solution.py:38
  77.2 5.0 %collective-permute-done.21.refs_11_ = bf16[512,896]{1,0:T(8,128)(2,1)S(1)} collective-permute-done((bf16[512,896]{1,0:T(8,128)(2,1)S(1)}, bf16[512,896]{1,0:T(8,128)(2,1)S(1)}, u32[]{:S(2)}, u32[]{:S(2)}) %collective-permute-start.21) | collective-permute-done | bytes 917536 | tf_op jit(solution)/shard_map/ppermute | solution.py:38
  82.3 5.8 %collective-permute-done.15.refs_15_.refs_7_.refs_10_ = bf16[512,1536]{1,0:T(8,128)(2,1)S(1)} collective-permute-done((bf16[512,1536]{1,0:T(8,128)(2,1)S(1)}, bf16[512,1536]{1,0:T(8,128)(2,1)S(1)}, u32[]{:S(2)}, u32[]{:S(2)}) %collective-permute-start.15) | collective-permute-done | bytes 1572896 | tf_op jit(solution)/shard_map/ppermute | solution.py:38
  88.1 5.8 %collective-permute-done.25.refs_3_ = bf16[256,1920]{1,0:T(8,128)(2,1)S(1)} collective-permute-done((bf16[256,1920]{1,0:T(8,128)(2,1)S(1)}, bf16[256,1920]{1,0:T(8,128)(2,1)S(1)}, u32[]{:S(2)}, u32[]{:S(2)}) %collective-permute-start.25) | collective-permute-done | bytes 983072 | tf_op jit(solution)/shard_map/ppermute | solution.py:38
  106.8 16.2 %shard_map.239 = (f32[256,1920]{1,0:T(8,128)}, bf16[256,1024]{1,0:T(8,128)(2,1)S(1)}, bf16[256,1024]{1,0:T(8,128)(2,1)S(1)}, bf16[256,1440]{1,0:T(8,128)(2,1)}, f32[8,1920]{1,0:T(8,128)S(1)}) custom-call(s32[1]{0:T(128)S(6)} %copy.26.refs_0_, bf16[256,1920]{1,0:T(8,128)(2,1)} %bitcast.29, s32[256,1]{1,0:T(8,128)S(1)} %get-tuple-element.167.refs_2_.left, ...), custom_call_target="tpu_custom_call" | custom-call | flops 8000000000 | bytes 19038212 | tf_op jit(solution)/shard_map/pallas_call | solution.py:52
  124.5 5.0 %all-to-all-start = ((bf16[32,8,1440]{2,1,0:T(8,128)(2,1)}), bf16[32,8,1440]{2,1,0:T(8,128)(2,1)S(1)}, u32[]{:S(2)}, u32[]{:S(2)}) async-start(bf16[32,8,1440]{2,1,0:T(8,128)(2,1)} %bitcast.26), calls=%async_computation | async-start | bytes 1572864 | tf_op jit(solution)/shard_map/all_to_all | solution.py:767
  134.0 11.5 %all-to-all-done = bf16[32,8,1440]{2,1,0:T(8,128)(2,1)S(1)} async-done(((bf16[32,8,1440]{2,1,0:T(8,128)(2,1)}), bf16[32,8,1440]{2,1,0:T(8,128)(2,1)S(1)}, u32[]{:S(2)}, u32[]{:S(2)}) %all-to-all-start) | async-done | bytes 737312 | tf_op jit(solution)/shard_map/all_to_all | solution.py:767
  147.8 7.1 %collective-permute-done.30.refs_12_ = bf16[512,384]{1,0:T(8,128)(2,1)} collective-permute-done((bf16[512,384]{1,0:T(8,128)(2,1)}, bf16[512,384]{1,0:T(8,128)(2,1)}, u32[]{:S(2)}, u32[]{:S(2)}) %collective-permute-start.30) | collective-permute-done | bytes 393248 | tf_op jit(solution)/shard_map/ppermute | solution.py:42
  155.0 6.7 %all-to-all-start.1 = ((bf16[32,8,480]{2,1,0:T(8,128)(2,1)}), bf16[32,8,480]{2,1,0:T(8,128)(2,1)S(1)}, u32[]{:S(2)}, u32[]{:S(2)}) async-start(bf16[32,8,480]{2,1,0:T(8,128)(2,1)} %bitcast.6), calls=%async_computation.1 | async-start | bytes 524288 | tf_op jit(solution)/shard_map/all_to_all | solution.py:767
  162.0 10.4 %all-to-all-done.1 = bf16[32,8,480]{2,1,0:T(8,128)(2,1)S(1)} async-done(((bf16[32,8,480]{2,1,0:T(8,128)(2,1)}), bf16[32,8,480]{2,1,0:T(8,128)(2,1)S(1)}, u32[]{:S(2)}, u32[]{:S(2)}) %all-to-all-start.1) | async-done | bytes 245792 | tf_op jit(solution)/shard_map/all_to_all | solution.py:767
  173.1 45.3 %shard_map.241 = (bf16[256,1920]{1,0:T(8,128)(2,1)}, f32[256,1920]{1,0:T(8,128)}, bf16[256,1024]{1,0:T(8,128)(2,1)}, bf16[256,1024]{1,0:T(8,128)(2,1)}, bf16[256...) custom-call(bf16[256,480]{1,0:T(8,128)(2,1)} %bitcast.28, ...), custom_call_target="tpu_custom_call" | custom-call | flops 24999999488 | bytes 34627584 | tf_op jit(solution)/shard_map/pallas_call | solution.py:52
  238.2 4.8 %all-to-all-start.2 = ((bf16[32,8,480]{2,1,0:T(8,128)(2,1)}), bf16[32,8,480]{2,1,0:T(8,128)(2,1)S(1)}, u32[]{:S(2)}, u32[]{:S(2)}) async-start(bf16[32,8,480]{2,1,0:T(8,128)(2,1)} %bitcast.27), calls=%async_computation.2 | async-start | bytes 524288 | tf_op jit(solution)/shard_map/all_to_all | solution.py:767
  243.4 23.1 %all-to-all-done.2 = bf16[32,8,480]{2,1,0:T(8,128)(2,1)S(1)} async-done(((bf16[32,8,480]{2,1,0:T(8,128)(2,1)}), bf16[32,8,480]{2,1,0:T(8,128)(2,1)S(1)}, u32[]{:S(2)}, u32[]{:S(2)}) %all-to-all-start.2) | async-done | bytes 245792 | tf_op jit(solution)/shard_map/all_to_all | solution.py:767
  268.5 6.7 %all-to-all-start.3 = ((bf16[32,8,1536]{2,1,0:T(8,128)(2,1)}), bf16[32,8,1536]{2,1,0:T(8,128)(2,1)S(1)}, u32[]{:S(2)}, u32[]{:S(2)}) async-start(bf16[32,8,1536]{2,1,0:T(8,128)(2,1)} %bitcast.12), calls=%async_computation.3 | async-start | bytes 1572864 | tf_op jit(solution)/shard_map/all_to_all | solution.py:767
  282.7 10.2 %collective-permute-done.38.refs_2_.refs_3_ = bf16[512,512]{1,0:T(8,128)(2,1)S(1)} collective-permute-done((bf16[512,512]{1,0:T(8,128)(2,1)S(1)}, bf16[512,512]{1,0:T(8,128)(2,1)S(1)}, u32[]{:S(2)}, u32[]{:S(2)}) %collective-permute-start.38) | collective-permute-done | bytes 524320 | tf_op jit(solution)/shard_map/ppermute | solution.py:38
  307.2 14.2 %shard_map.248 = (f32[256,1920]{1,0:T(8,128)}, bf16[256,1024]{1,0:T(8,128)(2,1)S(1)}, bf16[256,896]{1,0:T(8,128)(2,1)S(1)}, bf16[128,128]{1,0:T(8,128)(2,1)S(1)}) custom-call(s32[1]{0:T(128)S(6)} %copy.26.refs_0_, bf16[256,1536]{1,0:T(8,128)(2,1)S(1)} %bitcast.21, f32[256,1920]{1,0:T(8,128)} %get-tuple-element.214.refs_1_.refs_2_, ...), custom_call_target="tpu_custom_call" | custom-call | flops 6000000000 | bytes 14199812 | tf_op jit(solution)/shard_map/pallas_call | solution.py:52
  335.6 14.6 %collective-permute-done.54.refs_10_.refs_11_ = bf16[512,1024]{1,0:T(8,128)(2,1)S(1)} collective-permute-done((bf16[512,1024]{1,0:T(8,128)(2,1)S(1)}, bf16[512,1024]{1,0:T(8,128)(2,1)S(1)}, u32[]{:S(2)}, u32[]{:S(2)}) %collective-permute-start.54) | collective-permute-done | bytes 1048608 | tf_op jit(solution)/shard_map/ppermute | solution.py:38
  351.2 6.8 %collective-permute-done.51.refs_6_.refs_7_ = bf16[512,1024]{1,0:T(8,128)(2,1)S(1)} collective-permute-done((bf16[512,1024]{1,0:T(8,128)(2,1)S(1)}, bf16[512,1024]{1,0:T(8,128)(2,1)S(1)}, u32[]{:S(2)}, u32[]{:S(2)}) %collective-permute-start.51) | collective-permute-done | bytes 1048608 | tf_op jit(solution)/shard_map/ppermute | solution.py:38
  364.3 8.3 %collective-permute-done.57.refs_14_.refs_15_ = bf16[256,1024]{1,0:T(8,128)(2,1)S(1)} collective-permute-done((bf16[256,1024]{1,0:T(8,128)(2,1)S(1)}, bf16[256,1024]{1,0:T(8,128)(2,1)S(1)}, u32[]{:S(2)}, u32[]{:S(2)}) %collective-permute-start.57) | collective-permute-done | bytes 524320 | tf_op jit(solution)/shard_map/ppermute | solution.py:38
  386.1 8.7 %collective-permute-done.60.refs_2_.refs_3_ = bf16[128,2048]{1,0:T(8,128)(2,1)S(1)} collective-permute-done((bf16[128,2048]{1,0:T(8,128)(2,1)S(1)}, bf16[128,2048]{1,0:T(8,128)(2,1)S(1)}, u32[]{:S(2)}, u32[]{:S(2)}) %collective-permute-start.60) | collective-permute-done | bytes 524320 | tf_op jit(solution)/shard_map/ppermute | solution.py:38
  397.8 8.4 %collective-permute-done.63.refs_2_.refs_3_ = bf16[64,2048]{1,0:T(8,128)(2,1)S(1)} collective-permute-done((bf16[64,2048]{1,0:T(8,128)(2,1)S(1)}, bf16[64,2048]{1,0:T(8,128)(2,1)S(1)}, u32[]{:S(2)}, u32[]{:S(2)}) %collective-permute-start.63) | collective-permute-done | bytes 262176 | tf_op jit(solution)/shard_map/ppermute | solution.py:38
  (287 shorter events, 168.6 us)
Async XLA Ops:
  64.2 23.9 %collective-permute-start.15 = (bf16[512,1536]{1,0:T(8,128)(2,1)S(1)}, bf16[512,1536]{1,0:T(8,128)(2,1)S(1)}, u32[]{:S(2)}, u32[]{:S(2)}) collective-permute-start(bf16[512,1536]{1,0:T(8,128)(2,1)S(1)} %get-tuple-element.205.refs_14_.refs_6_.refs_9_), channel_id=1, source_target_pairs={{0,80},{1,81},{2,82},{3,83},{4,84},{5,85},{6,86},{7,87},{8,88},{9,... | collective-permute-start | bytes 4718600 | tf_op jit(solution)/shard_map/ppermute | solution.py:38
  69.1 28.1 %collective-permute-start.18 = (bf16[512,1024]{1,0:T(8,128)(2,1)S(1)}, bf16[512,1024]{1,0:T(8,128)(2,1)S(1)}, u32[]{:S(2)}, u32[]{:S(2)}) collective-permute-start(bf16[512,1024]{1,0:T(8,128)(2,1)S(1)} %get-tuple-element.197.refs_6_), channel_id=1, source_target_pairs={{0,3},{1,2},{2,1},{3,0},{4,7},{5,6},{6,5},{7,4},{8,11},{9,10},{10,... | collective-permute-start | bytes 3145736 | tf_op jit(solution)/shard_map/ppermute | solution.py:38
  102.3 44.8 %collective-permute-start.28 = (bf16[512,1920]{1,0:T(8,128)(2,1)S(1)}, bf16[512,1920]{1,0:T(8,128)(2,1)}, u32[]{:S(2)}, u32[]{:S(2)}) collective-permute-start(bf16[512,1920]{1,0:T(8,128)(2,1)S(1)} %get-tuple-element.211.refs_14_), channel_id=1, source_target_pairs={{0,3},{1,2},{2,1},{3,0},{4,7},{5,6},{6,5},{7,4},{8,11},{9,10},{10,... | collective-permute-start | bytes 5898248 | tf_op jit(solution)/shard_map/ppermute | solution.py:38
  105.6 41.5 %collective-permute-start.29 = (bf16[512,1920]{1,0:T(8,128)(2,1)}, bf16[512,1920]{1,0:T(8,128)(2,1)}, u32[]{:S(2)}, u32[]{:S(2)}) collective-permute-start(bf16[512,1920]{1,0:T(8,128)(2,1)} %get-tuple-element.212.refs_18_), channel_id=1, source_target_pairs={{0,12},{1,13},{2,14},{3,15},{4,8},{5,9},{6,10},{7,11},{8,4},{9,5},... | collective-permute-start | bytes 5898248 | tf_op jit(solution)/shard_map/ppermute | solution.py:38
  124.5 21.0 %all-to-all-start = ((bf16[32,8,1440]{2,1,0:T(8,128)(2,1)}), bf16[32,8,1440]{2,1,0:T(8,128)(2,1)S(1)}, u32[]{:S(2)}, u32[]{:S(2)}) async-start(bf16[32,8,1440]{2,1,0:T(8,128)(2,1)} %bitcast.26), calls=%async_computation | async-start | bytes 1572864 | tf_op jit(solution)/shard_map/all_to_all | solution.py:767
  129.5 17.6 %collective-permute-start.27 = (bf16[512,384]{1,0:T(8,128)(2,1)}, bf16[512,384]{1,0:T(8,128)(2,1)}, u32[]{:S(2)}, u32[]{:S(2)}) collective-permute-start(bf16[512,384]{1,0:T(8,128)(2,1)} %copy-done.32), channel_id=1, source_target_pairs={{0,80},{1,81},{2,82},{3,83},{4,84},{5,85},{6,86},{7,87},{8,88},{9,... | collective-permute-start | bytes 1179656 | tf_op jit(solution)/shard_map/ppermute | solution.py:38
  133.4 28.3 %collective-permute-start.32 = (bf16[512,1920]{1,0:T(8,128)(2,1)S(1)}, bf16[512,1920]{1,0:T(8,128)(2,1)}, u32[]{:S(2)}, u32[]{:S(2)}) collective-permute-start(bf16[512,1920]{1,0:T(8,128)(2,1)S(1)} %get-tuple-element.211.refs_14_), channel_id=1, source_target_pairs={{0,32},{1,33},{2,34},{3,35},{4,36},{5,37},{6,38},{7,39},{8,40},{9,... | collective-permute-start | bytes 5898248 | tf_op jit(solution)/shard_map/ppermute | solution.py:42
  133.4 28.6 %collective-permute-start.34 = (bf16[512,1920]{1,0:T(8,128)(2,1)}, bf16[512,1920]{1,0:T(8,128)(2,1)}, u32[]{:S(2)}, u32[]{:S(2)}) collective-permute-start(bf16[512,1920]{1,0:T(8,128)(2,1)} %get-tuple-element.212.refs_18_), channel_id=1, source_target_pairs={{0,32},{1,33},{2,34},{3,35},{4,36},{5,37},{6,38},{7,39},{8,40},{9,... | collective-permute-start | bytes 5898248 | tf_op jit(solution)/shard_map/ppermute | solution.py:42
  147.1 25.4 %collective-permute-start.33 = (bf16[512,1920]{1,0:T(8,128)(2,1)}, bf16[512,1920]{1,0:T(8,128)(2,1)}, u32[]{:S(2)}, u32[]{:S(2)}) collective-permute-start(bf16[512,1920]{1,0:T(8,128)(2,1)} %collective-permute-done.28.refs_15_), channel_id=1, source_target_pairs={{0,32},{1,33},{2,34},{3,35},{4,36},{5,37},{6,38},{7,39},{8,40},{9,... | collective-permute-start | bytes 5898248 | tf_op jit(solution)/shard_map/ppermute | solution.py:42
  147.2 25.3 %collective-permute-start.35 = (bf16[512,1920]{1,0:T(8,128)(2,1)}, bf16[512,1920]{1,0:T(8,128)(2,1)}, u32[]{:S(2)}, u32[]{:S(2)}) collective-permute-start(bf16[512,1920]{1,0:T(8,128)(2,1)} %collective-permute-done.29.refs_19_), channel_id=1, source_target_pairs={{0,32},{1,33},{2,34},{3,35},{4,36},{5,37},{6,38},{7,39},{8,40},{9,... | collective-permute-start | bytes 5898248 | tf_op jit(solution)/shard_map/ppermute | solution.py:42
  154.9 17.6 %collective-permute-start.31 = (bf16[512,384]{1,0:T(8,128)(2,1)}, bf16[512,384]{1,0:T(8,128)(2,1)}, u32[]{:S(2)}, u32[]{:S(2)}) collective-permute-start(bf16[512,384]{1,0:T(8,128)(2,1)} %collective-permute-done.27.refs_11_), channel_id=1, source_target_pairs={{0,32},{1,33},{2,34},{3,35},{4,36},{5,37},{6,38},{7,39},{8,40},{9,... | collective-permute-start | bytes 1179656 | tf_op jit(solution)/shard_map/ppermute | solution.py:42
  155.0 17.4 %all-to-all-start.1 = ((bf16[32,8,480]{2,1,0:T(8,128)(2,1)}), bf16[32,8,480]{2,1,0:T(8,128)(2,1)S(1)}, u32[]{:S(2)}, u32[]{:S(2)}) async-start(bf16[32,8,480]{2,1,0:T(8,128)(2,1)} %bitcast.6), calls=%async_computation.1 | async-start | bytes 524288 | tf_op jit(solution)/shard_map/all_to_all | solution.py:767
  161.8 57.6 %collective-permute-start.43 = (bf16[256,1920]{1,0:T(8,128)(2,1)}, bf16[256,1920]{1,0:T(8,128)(2,1)S(1)}, u32[]{:S(2)}, u32[]{:S(2)}) collective-permute-start(bf16[256,1920]{1,0:T(8,128)(2,1)} %bitcast.23), channel_id=1, source_target_pairs={{0,32},{1,33},{2,34},{3,35},{4,36},{5,37},{6,38},{7,39},{8,40},{9,... | collective-permute-start | bytes 2949128 | tf_op jit(solution)/shard_map/ppermute | solution.py:42
  230.1 62.8 %collective-permute-start.44 = (bf16[512,1920]{1,0:T(8,128)(2,1)S(1)}, bf16[512,1920]{1,0:T(8,128)(2,1)}, u32[]{:S(2)}, u32[]{:S(2)}) collective-permute-start(bf16[512,1920]{1,0:T(8,128)(2,1)S(1)} %get-tuple-element.235), channel_id=1, source_target_pairs={{0,12},{1,13},{2,14},{3,15},{4,8},{5,9},{6,10},{7,11},{8,4},{9,5},... | collective-permute-start | bytes 5898248 | tf_op jit(solution)/shard_map/ppermute | solution.py:38
  236.6 56.3 %collective-permute-start.41 = (bf16[512,1920]{1,0:T(8,128)(2,1)}, bf16[512,1920]{1,0:T(8,128)(2,1)}, u32[]{:S(2)}, u32[]{:S(2)}) collective-permute-start(bf16[512,1920]{1,0:T(8,128)(2,1)} %get-tuple-element.231), channel_id=1, source_target_pairs={{0,3},{1,2},{2,1},{3,0},{4,7},{5,6},{6,5},{7,4},{8,11},{9,10},{10,... | collective-permute-start | bytes 5898248 | tf_op jit(solution)/shard_map/ppermute | solution.py:38
  238.2 37.0 %collective-permute-start.36 = (bf16[256,1024]{1,0:T(8,128)(2,1)}, bf16[256,1024]{1,0:T(8,128)(2,1)}, u32[]{:S(2)}, u32[]{:S(2)}) collective-permute-start(bf16[256,1024]{1,0:T(8,128)(2,1)} %get-tuple-element.223), channel_id=1, source_target_pairs={{0,32},{1,33},{2,34},{3,35},{4,36},{5,37},{6,38},{7,39},{8,40},{9,... | collective-permute-start | bytes 1572872 | tf_op jit(solution)/shard_map/ppermute | solution.py:42
  238.2 28.2 %all-to-all-start.2 = ((bf16[32,8,480]{2,1,0:T(8,128)(2,1)}), bf16[32,8,480]{2,1,0:T(8,128)(2,1)S(1)}, u32[]{:S(2)}, u32[]{:S(2)}) async-start(bf16[32,8,480]{2,1,0:T(8,128)(2,1)} %bitcast.27), calls=%async_computation.2 | async-start | bytes 524288 | tf_op jit(solution)/shard_map/all_to_all | solution.py:767
  243.1 32.1 %collective-permute-start.37 = (bf16[256,512]{1,0:T(8,128)(2,1)}, bf16[256,512]{1,0:T(8,128)(2,1)}, u32[]{:S(2)}, u32[]{:S(2)}) collective-permute-start(bf16[256,512]{1,0:T(8,128)(2,1)} %get-tuple-element.224.right), channel_id=1, source_target_pairs={{0,32},{1,33},{2,34},{3,35},{4,36},{5,37},{6,38},{7,39},{8,40},{9,... | collective-permute-start | bytes 786440 | tf_op jit(solution)/shard_map/ppermute | solution.py:42
  268.5 30.9 %all-to-all-start.3 = ((bf16[32,8,1536]{2,1,0:T(8,128)(2,1)}), bf16[32,8,1536]{2,1,0:T(8,128)(2,1)S(1)}, u32[]{:S(2)}, u32[]{:S(2)}) async-start(bf16[32,8,1536]{2,1,0:T(8,128)(2,1)} %bitcast.12), calls=%async_computation.3 | async-start | bytes 1572864 | tf_op jit(solution)/shard_map/all_to_all | solution.py:767
  322.0 36.0 %collective-permute-start.48 = (bf16[512,1536]{1,0:T(8,128)(2,1)S(1)}, bf16[512,1536]{1,0:T(8,128)(2,1)S(1)}, u32[]{:S(2)}, u32[]{:S(2)}) collective-permute-start(bf16[512,1536]{1,0:T(8,128)(2,1)S(1)} %get-tuple-element.254), channel_id=1, source_target_pairs={{0,80},{1,81},{2,82},{3,83},{4,84},{5,85},{6,86},{7,87},{8,88},{9,... | collective-permute-start | bytes 4718600 | tf_op jit(solution)/shard_map/ppermute | solution.py:38
  328.2 22.0 %collective-permute-start.54 = (bf16[512,1024]{1,0:T(8,128)(2,1)S(1)}, bf16[512,1024]{1,0:T(8,128)(2,1)S(1)}, u32[]{:S(2)}, u32[]{:S(2)}) collective-permute-start(bf16[512,1024]{1,0:T(8,128)(2,1)S(1)} %get-tuple-element.261), channel_id=1, source_target_pairs={{0,12},{1,13},{2,14},{3,15},{4,8},{5,9},{6,10},{7,11},{8,4},{9,5},... | collective-permute-start | bytes 3145736 | tf_op jit(solution)/shard_map/ppermute | solution.py:38
  332.7 25.4 %collective-permute-start.51 = (bf16[512,1024]{1,0:T(8,128)(2,1)S(1)}, bf16[512,1024]{1,0:T(8,128)(2,1)S(1)}, u32[]{:S(2)}, u32[]{:S(2)}) collective-permute-start(bf16[512,1024]{1,0:T(8,128)(2,1)S(1)} %get-tuple-element.257), channel_id=1, source_target_pairs={{0,3},{1,2},{2,1},{3,0},{4,7},{5,6},{6,5},{7,4},{8,11},{9,10},{10,... | collective-permute-start | bytes 3145736 | tf_op jit(solution)/shard_map/ppermute | solution.py:38
  335.2 29.1 %collective-permute-start.56 = (bf16[256,1920]{1,0:T(8,128)(2,1)S(1)}, bf16[256,1920]{1,0:T(8,128)(2,1)S(1)}, u32[]{:S(2)}, u32[]{:S(2)}) collective-permute-start(bf16[256,1920]{1,0:T(8,128)(2,1)S(1)} %get-tuple-element.265), channel_id=1, source_target_pairs={{0,1},{1,0},{2,3},{3,2},{4,5},{5,4},{6,7},{7,6},{8,9},{9,8},{10,11... | collective-permute-start | bytes 2949128 | tf_op jit(solution)/shard_map/ppermute | solution.py:38
  335.4 28.8 %collective-permute-start.58 = (bf16[256,1920]{1,0:T(8,128)(2,1)S(1)}, bf16[256,1920]{1,0:T(8,128)(2,1)S(1)}, u32[]{:S(2)}, u32[]{:S(2)}) collective-permute-start(bf16[256,1920]{1,0:T(8,128)(2,1)S(1)} %get-tuple-element.269), channel_id=1, source_target_pairs={{0,4},{1,5},{2,6},{3,7},{4,0},{5,1},{6,2},{7,3},{8,12},{9,13},{10,... | collective-permute-start | bytes 2949128 | tf_op jit(solution)/shard_map/ppermute | solution.py:38
  (117 other events, 1212.5 us)

commit v2 on v1

--- a/solution.py
+++ b/solution.py
@@ -42,7 +42,7 @@
     return lax.ppermute(value, AXES, [(i, i ^ CORE_BIT) for i in range(SHARDS)])
 
 
-def call(kernel, out_shape, vmem=32, flops=0, **options):
+def call(kernel, out_shape, vmem=60, flops=0, **options):
     params = pltpu.CompilerParams(vmem_limit_bytes=vmem * MIB)
 
     def run(*args):
@@ -157,7 +157,6 @@
     out = call(
         functools.partial(add_kernel, [len(group) for group in groups]),
         tuple(shape(rows, width) for width in widths for _ in range(2)),
-        vmem=48,
         grid=(tiles,),
         in_specs=specs,
         out_specs=tuple(pl.BlockSpec((tile, width), lambda i: (i, 0)) for width in widths for _ in range(2)),
@@ -165,51 +164,82 @@
     return [(out[2 * i], out[2 * i + 1]) for i in range(len(groups))]
 
 
-def outer_kernel(tiles, line, extra, left, left_got, right, right_got, *refs):
+def store_group(order, group, kept, sent, span, total):
+    if order == 0:
+
+        @pl.when(group < 2)
+        def _():
+            kept[pl.ds(pl.multiple_of(group * 256, 256), 256), span] = total
+
+        @pl.when(group >= 2)
+        def _():
+            sent[pl.ds(pl.multiple_of((group - 2) * 256, 256), 256), span] = total
+
+    for number in range(4 if order == 1 else 16 if order == 2 else 0):
+        rows = 64 if order == 1 else ROWS
+        half, offset = piece_place(order, number)
+        start = pl.multiple_of(offset + group * rows, ROWS)
+        (kept, sent)[half][pl.ds(start, rows), span] = total[number * rows : number * rows + rows]
+
+
+def piece_place(order, number):
+    if order == 1:
+        return number >> 1, 256 * (number & 1)
+    return number >> 3, 256 * ((number >> 2) & 1) + 64 * (number & 3)
+
+
+def outer_kernel(order, left, left_got, right, right_got, kept, sent):
+    group = pl.program_id(0)
+    columns = right.shape[1]
+    one, two = left[...], left_got[...]
+    for cut in range(0, columns, 512):
+        span = slice(cut, min(cut + 512, columns))
+        total = rows_dot(one, right[:, span]) + rows_dot(two, right_got[:, span])
+        store_group(order, group, kept, sent, span, total.astype(bf16))
+
+
+def outer(order, left, left_got, right, right_got):
+    columns = right.shape[1]
+    outs = (shape(HALF // 2, columns), shape(HALF // 2, columns))
+    group = pl.BlockSpec((TOKENS, 256), lambda i: (0, i))
+    return call(
+        functools.partial(outer_kernel, order),
+        outs,
+        flops=2 * 512 * HALF * columns,
+        grid=(4,),
+        in_specs=[group, group, whole(right), whole(right_got)],
+        out_specs=tuple(whole(v) for v in outs),
+    )(left, left_got, right, right_got)
+
+
+def table_kernel(line, small, codes, codes_got, right, right_got, targets, *refs):
     kept, sent = refs[-2:]
-    rows = HALF // 2 // tiles
     columns = right.shape[1]
     step = pl.program_id(0)
     for target, base in ((kept, 0), (sent, HALF // 2)):
-        start = pl.multiple_of(base + step * rows, rows)
-        if line is None:
-            one, two = left[:, pl.ds(start, rows)], left_got[:, pl.ds(start, rows)]
-        else:
-            places_here = refs[0][line : line + 1, pl.ds(start, rows)]
-            one, two = hot(left[...], places_here), hot(left_got[...], places_here)
+        start = pl.multiple_of(base + step * 256, 256)
+        here = targets[line : line + 1, pl.ds(start, 256)]
+        one, two = hot(codes[...], here), hot(codes_got[...], here)
         for cut in range(0, columns, 512):
             span = slice(cut, min(cut + 512, columns))
             total = rows_dot(one, right[:, span]) + rows_dot(two, right_got[:, span])
             target[:, span] = total.astype(bf16)
-        if extra == "small":
-            row = lax.broadcasted_iota(jnp.int32, (rows, 64), 0) + start
-            chunk = lax.broadcasted_iota(jnp.int32, (rows, 64), 1)
-            target[:, columns:] = dot(hot(row, chunk * ROWS), refs[1][...]).astype(bf16)
-        elif extra == "zero":
-            target[:, columns:] = jnp.zeros((rows, target.shape[1] - columns), bf16)
-
-
-def outer(left, left_got, right, right_got, line=None, targets=None, small=None):
-    tiles = 4
-    args = (left, left_got, right, right_got)
-    columns = right.shape[1]
-    extra = None
-    if line is not None:
-        args += (targets,)
-    if small is not None:
-        args += (small,)
-        extra = "small"
-        columns += 128
-    elif columns % 128:
-        extra = "zero"
-        columns += 128 - columns % 128
+        if small:
+            row = lax.broadcasted_iota(jnp.int32, (256, 64), 0) + start
+            chunk = lax.broadcasted_iota(jnp.int32, (256, 64), 1)
+            target[:, columns:] = dot(hot(row, chunk * ROWS), refs[0][...]).astype(bf16)
+
+
+def table_outer(line, codes, codes_got, right, right_got, targets, small=None):
+    args = (codes, codes_got, right, right_got, targets) + (() if small is None else (small,))
+    columns = right.shape[1] + (0 if small is None else 128)
     half = shape(HALF // 2, columns)
-    tile = pl.BlockSpec((HALF // 2 // tiles, columns), lambda i: (i, 0))
-    return call(
-        functools.partial(outer_kernel, tiles, line, extra),
+    tile = pl.BlockSpec((256, columns), lambda i: (i, 0))
+    return call(
+        functools.partial(table_kernel, line, small is not None),
         (half, half),
         flops=2 * 512 * HALF * columns,
-        grid=(tiles,),
+        grid=(2,),
         in_specs=[whole(v) for v in args],
         out_specs=(tile, tile),
     )(*args)
@@ -217,6 +247,8 @@
 
 def shard_tables():
     table = np.zeros((2, 8, SHARDS), np.int32)
+    groups = np.zeros((2, 8, 16), np.int32)
+    inside = (("x", "z"), ("z", "x"), ("x", "z"))
     for core in range(2):
         for number, order in enumerate(ORDERS):
             for place in range(SHARDS):
@@ -226,9 +258,16 @@
                     if (place >> step) & 1:
                         mask ^= STEP_BITS[order[step // 2]][(step % 2) ^ here]
                 table[core, number, place] = mask
+            for half in range(2):
+                for place in range(16):
+                    mask = 0
+                    for step in range(4):
+                        if (place >> step) & 1:
+                            mask ^= STEP_BITS[inside[number][step // 2]][(step % 2) ^ core ^ half]
+                    groups[core, 2 * number + half, place] = mask
     table[:, 3:5] = table[:, 1:3]
     lines = np.repeat(table, ROWS, axis=2)
-    return lines, lines.transpose(0, 2, 1).copy(), table.transpose(0, 2, 1).copy()
+    return lines, np.repeat(groups, ROWS, axis=2), table.transpose(0, 2, 1).copy()
 
 
 def prepare_kernel(qkv, attn, expand, reduce, table, gain, shift, level, *outs):
@@ -259,19 +298,14 @@
     )(*args)
 
 
-def places_kernel(here, codes_line, lines, columns, shards, targets, target_columns, shard_column, codes):
+def places_kernel(here, codes_line, lines, groups, shards, targets, offsets, shard_column, codes):
     me, core = here[0], here[1]
-
-    def feature_of(place, inside):
-        return jnp.where(inside < 15, place * 15 + inside, -1)
-
     place = jnp.where(core == 0, lines[0], lines[1]) ^ me
     inside = lax.broadcasted_iota(jnp.int32, place.shape, 1) & 15
-    line = lax.broadcasted_iota(jnp.int32, place.shape, 0)
-    targets[...] = jnp.where(line < 3, feature_of(place, inside), place * 16 + inside)
-    place = jnp.where(core == 0, columns[0], columns[1]) ^ me
-    inside = lax.broadcasted_iota(jnp.int32, place.shape, 0) & 15
-    target_columns[...] = feature_of(place, inside)
+    targets[...] = place * 16 + inside
+    place = jnp.where(core == 0, groups[0], groups[1]) ^ (me & 15)
+    inside = lax.broadcasted_iota(jnp.int32, place.shape, 1) & 15
+    offsets[...] = jnp.where(inside < 15, place * 15 + inside, -8192)
     shard_column[...] = jnp.where(core == 0, shards[0], shards[1]) ^ me
     row = jnp.right_shift(lax.broadcasted_iota(jnp.int32, (TOKENS, 64), 0), 2)
     column = lax.broadcasted_iota(jnp.int32, (TOKENS, 64), 1)
@@ -282,7 +316,7 @@
 def places(here, codes_line):
     i32 = jnp.int32
     args = (codes_line, *(jnp.asarray(t) for t in shard_tables()))
-    outs = (shape(8, 2048, i32), shape(2048, 8, i32), shape(SHARDS, 8, i32), shape(TOKENS, 1, i32))
+    outs = (shape(8, 2048, i32), shape(8, 256, i32), shape(SHARDS, 8, i32), shape(TOKENS, 1, i32))
     return call(
         places_kernel,
         outs,
@@ -338,29 +372,69 @@
         body(pl.ds(pl.multiple_of(i * ROW_STEP, ROW_STEP), ROW_STEP))
 
 
-def shuffle(value, targets, line, own, other):
+def group_window(here, offsets, order, half, group):
+    core = here[1] ^ half
+    number = jnp.right_shift(here[0], 4) ^ (2 * half)
+    number = number ^ ((group & 1) * (4 + core)) ^ (jnp.right_shift(group, 1) * (5 - core))
+    first = number * 240
+    start = jnp.minimum(jnp.right_shift(first, 7) * 128, D - 384)
+    line = 2 * order + half
+    feature = lax.broadcasted_iota(jnp.int32, (384, 256), 0)
+    return pl.ds(pl.multiple_of(start, 128), 384), hot(feature, offsets[line : line + 1, :] + (first - start))
+
+
+def slot(group):
+    return pl.ds(pl.multiple_of(group * 256, 256), 256)
+
+
+def shuffle(here, offsets, order, value, own, other):
     for half, target in enumerate((own, other)):
 
-        def part(span, half=half, target=target):
-            place = targets[line : line + 1, pl.ds(pl.multiple_of(span.start + half * HALF, 128), 256)]
-            feature = lax.broadcasted_iota(jnp.int32, (D, 256), 0)
-            target[:, span] = dot(value[...], hot(feature, place)).astype(bf16)
-
-        each_chunk(HALF, part, 256)
-
-
-def unshuffle(value, target_columns, line, out):
-    def part(span):
-        feature = lax.broadcasted_iota(jnp.int32, (512, CHUNK), 1) + span.start
-        total = None
-        for k in range(4):
-            cut = slice(512 * k, 512 * k + 512)
-            place = target_columns[cut, line : line + 1]
-            term = dot(value[:, cut], hot(place, feature))
+        @pl.loop(0, 4)
+        def _(group, half=half, target=target):
+            window, chosen = group_window(here, offsets, order, half, group)
+            target[:, slot(group)] = dot(value[:, window], chosen).astype(bf16)
+
+
+def unshuffle(here, offsets, order, value, out):
+    out[...] = jnp.zeros(out.shape, f32)
+    for half in range(2):
+
+        @pl.loop(0, 4)
+        def _(group, half=half):
+            window, chosen = group_window(here, offsets, order, half, group)
+            out[:, window] += cols_dot(value[:, slot(group + 4 * half)], chosen)
+
+
+def group_rows(order, pieces, half, group, span=slice(None)):
+    if order == 0:
+        raise NotImplementedError
+    rows = 64 if order == 1 else ROWS
+    parts = []
+    for number in range(256 // rows):
+        piece, offset = piece_place(order, number)
+        start = offset + group * rows
+        start = start if isinstance(start, int) else pl.multiple_of(start, ROWS)
+        parts.append(pieces[2 * half + piece][pl.ds(start, rows), span])
+    return jnp.concatenate(parts, axis=0)
+
+
+def group_sum(order, own, other, pieces, span):
+    total = None
+    for half, value in enumerate((own, other)):
+        for group in range(4):
+            term = dot(value[:, slice(group * 256, group * 256 + 256)], group_rows(order, pieces, half, group, span))
             total = term if total is None else total + term
-        out[:, span] = total
-
-    each_chunk(D, part)
+    return total
+
+
+def group_back(order, value, pieces, wide):
+    for half in range(2):
+
+        @pl.loop(0, 4)
+        def _(group, half=half):
+            term = cols_dot(value[...], group_rows(order, pieces, half, group))
+            wide[:, slot(group + 4 * half)] = term.astype(bf16)
 
 
 def pieces_of(own, other):
@@ -391,8 +465,8 @@
 
 
 def embed_kernel(*refs):
-    small, big, outs, scratch = split_refs(refs, 6, 12, 5, len(refs) - 23)
-    level, hidden, codes, targets, shard_column, marks = small
+    small, big, outs, scratch = split_refs(refs, 8, 12, 5, len(refs) - 25)
+    here, level, hidden, codes, targets, offsets, shard_column, marks = small
     stream, own, other, packed, vectors = outs
     normed = scratch[-1]
     fetch = Fetch(big, scratch[:12], scratch[12])
@@ -429,13 +503,13 @@
 
     each_rows(rows)
     normed[...] = dot(row_move(), normed[...]).astype(bf16)
-    shuffle(normed, targets, 0, own, other)
+    shuffle(here, offsets, 0, normed, own, other)
     packed[...] = sum(dot(p, w[:, 0:1440]) for p, w in zip(pieces_of(own, other), weight)).astype(bf16)
 
 
-def embed(level, hidden, codes, targets, shard_column, marks, tables_a, tables_b, qkv):
+def embed(here, level, hidden, codes, targets, offsets, shard_column, marks, tables_a, tables_b, qkv):
     big = (*tables_a, *tables_b, *qkv)
-    args = (hidden, codes, targets, shard_column, marks)
+    args = (hidden, codes, targets, offsets, shard_column, marks)
     outs = (
         shape(TOKENS, D, f32),
         shape(TOKENS, HALF),
@@ -446,15 +520,14 @@
     return call(
         embed_kernel,
         outs,
-        vmem=52,
         flops=8e9,
         grid=(1,),
-        in_specs=[pl.BlockSpec(memory_space=pltpu.SMEM)]
+        in_specs=[pl.BlockSpec(memory_space=pltpu.SMEM)] * 2
         + [whole(v) for v in args]
         + [pl.BlockSpec(memory_space=pl.ANY)] * 12,
         out_specs=outs_whole(outs),
         scratch_shapes=fetched(big) + [pltpu.VMEM((TOKENS, D), bf16)],
-    )(level, *args, *big)
+    )(here, level, *args, *big)
 
 
 def probabilities(columns):
@@ -502,21 +575,27 @@
     )(columns, d_mixed)
 
 
-def middle_kernel(*refs):
-    small, big, outs, scratch = split_refs(refs, 6, 16, 12, len(refs) - 34)
-    mixed_columns, stream, vectors, upstream, targets, target_columns = small
-    block_out, d_mid, second_own, second_other, active_own, active_other = outs[:6]
-    attn_own, attn_other, d_upward, mixed, d_mixed, sums = outs[6:]
-    fetch = Fetch([ref.at[:, 1280:1536] for ref in big[:4]] + list(big[4:]), scratch[:16], scratch[16])
-    mid, work, slope, wide, low = scratch[17:]
-    rest, attn = fetch(*range(0, 4)), fetch(*range(4, 8))
+def cut_rest(pieces):
+    return [ref.at[:, 1280:1536] for ref in pieces]
+
+
+REST = [jax.ShapeDtypeStruct((512, 256), bf16)] * 4
+
+
+def rise_kernel(*refs):
+    small, big, outs, scratch = split_refs(refs, 5, 12, 7, len(refs) - 24)
+    here, mixed_columns, stream, vectors, offsets = small
+    mixed, mid, second_own, second_other, active_own, active_other, slope = outs
+    fetch = Fetch(cut_rest(big[:4]) + list(big[4:]), scratch[:12], scratch[12])
+    work, wide, low = scratch[13:]
     mixed[:, 480:512] = jnp.zeros((TOKENS, 32), bf16)
     mixed[:, 0:480] = dot(row_move(True), mixed_columns[...]).astype(bf16)
     end = tail_lanes(mixed[:, 0:480])
+    rest, attn = fetch(*range(0, 4)), fetch(*range(4, 8))
     for k in range(4):
         total = cols_dot(mixed[:, 0:384], attn[k][...]) + cols_dot(end, rest[k][...])
         wide[:, 512 * k : 512 * k + 512] = total.astype(bf16)
-    unshuffle(wide, target_columns, 0, work)
+    unshuffle(here, offsets, 0, wide, work)
 
     def rows_first(span):
         value = stream[span, :] + work[span, :]
@@ -525,12 +604,11 @@
         low[span, :] = (centered * scale * vectors[1:2, :] + vectors[3:4, :]).astype(bf16)
 
     each_rows(rows_first)
-    shuffle(low, targets, 1, second_own, second_other)
+    shuffle(here, offsets, 1, low, second_own, second_other)
     expand = fetch(*range(8, 12))
 
     def up(span):
-        parts = zip(pieces_of(second_own, second_other), expand)
-        work[:, span] = sum(dot(p, w[:, span]) for p, w in parts)
+        work[:, span] = group_sum(1, second_own, second_other, expand, span)
 
     each_chunk(D, up)
 
@@ -544,26 +622,82 @@
         slope[span, :] = 0.5 * (1.0 + bend) + 0.5 * value * (1.0 - bend * bend) * inner
 
     each_rows(rows_active)
-    shuffle(low, targets, 2, active_own, active_other)
-    reduce = fetch(*range(12, 16))
-
-    def down(span):
-        parts = zip(pieces_of(active_own, active_other), reduce)
-        total = sum(dot(p, w[:, span]) for p, w in parts)
-        block_out[:, span] = (mid[:, span] + total).astype(bf16)
-
-    each_chunk(D, down)
-    for k in range(4):
-        wide[:, 512 * k : 512 * k + 512] = cols_dot(upstream[...], reduce[k][...]).astype(bf16)
-    unshuffle(wide, target_columns, 2, work)
+    shuffle(here, offsets, 2, low, active_own, active_other)
+
+
+def rise(here, mixed_columns, stream, vectors, offsets, qkv, attn, expand):
+    big = (*qkv, *attn, *expand)
+    args = (mixed_columns, stream, vectors, offsets)
+    outs = (
+        (shape(TOKENS, 512), shape(TOKENS, D, f32))
+        + (shape(TOKENS, HALF),) * 4
+        + (shape(TOKENS, D, f32),)
+    )
+    return call(
+        rise_kernel,
+        outs,
+        flops=6e9,
+        grid=(1,),
+        in_specs=[pl.BlockSpec(memory_space=pltpu.SMEM)]
+        + [whole(v) for v in args]
+        + [pl.BlockSpec(memory_space=pl.ANY)] * 12,
+        out_specs=tuple(whole(v) for v in outs),
+        scratch_shapes=fetched(REST + list(big[4:]))
+        + [
+            pltpu.VMEM((TOKENS, D), f32),
+            pltpu.VMEM((TOKENS, 2 * HALF), bf16),
+            pltpu.VMEM((TOKENS, D), bf16),
+        ],
+    )(here, *args, *big)
+
+
+def turn_kernel(*refs):
+    small, big, outs, scratch = split_refs(refs, 7, 4, 2, len(refs) - 13)
+    here, mid, active_own, active_other, slope, upstream, offsets = small
+    block_out, d_upward = outs
+    fetch = Fetch(big, scratch[:4], scratch[4])
+    work, wide = scratch[5:]
+    reduce = fetch(*range(4))
+    group_back(2, upstream, reduce, wide)
+    unshuffle(here, offsets, 2, wide, work)
 
     def rows_upward(span):
         d_upward[span, :] = (slope[span, :] * work[span, :]).astype(bf16)
 
     each_rows(rows_upward)
-    for k in range(4):
-        wide[:, 512 * k : 512 * k + 512] = cols_dot(d_upward[...], expand[k][...]).astype(bf16)
-    unshuffle(wide, target_columns, 1, work)
+
+    def down(span):
+        total = group_sum(2, active_own, active_other, reduce, span)
+        block_out[:, span] = (mid[:, span] + total).astype(bf16)
+
+    each_chunk(D, down)
+
+
+def turn(here, mid, active_own, active_other, slope, upstream, offsets, reduce):
+    args = (mid, active_own, active_other, slope, upstream, offsets)
+    outs = (shape(TOKENS, D), shape(TOKENS, D))
+    return call(
+        turn_kernel,
+        outs,
+        flops=6e9,
+        grid=(1,),
+        in_specs=[pl.BlockSpec(memory_space=pltpu.SMEM)]
+        + [whole(v) for v in args]
+        + [pl.BlockSpec(memory_space=pl.ANY)] * 4,
+        out_specs=tuple(whole(v) for v in outs),
+        scratch_shapes=fetched(reduce)
+        + [pltpu.VMEM((TOKENS, D), f32), pltpu.VMEM((TOKENS, 2 * HALF), bf16)],
+    )(here, *args, *reduce)
+
+
+def fall_kernel(*refs):
+    small, big, outs, scratch = split_refs(refs, 6, 12, 5, len(refs) - 23)
+    here, d_upward, mid, upstream, vectors, offsets = small
+    d_mid, attn_own, attn_other, d_mixed, sums = outs
+    fetch = Fetch(list(big[:4]) + cut_rest(big[4:8]) + list(big[8:]), scratch[:12], scratch[12])
+    work, wide, low = scratch[13:]
+    group_back(1, d_upward, fetch(*range(0, 4)), wide)
+    unshuffle(here, offsets, 1, wide, work)
     sums[...] = jnp.zeros(sums.shape, f32)
 
     def rows_back(span):
@@ -576,7 +710,8 @@
         sums[1:2, :] += jnp.sum(grad, axis=0, keepdims=True)
 
     each_rows(rows_back)
-    shuffle(low, targets, 0, attn_own, attn_other)
+    shuffle(here, offsets, 0, low, attn_own, attn_other)
+    rest, attn = fetch(*range(4, 8)), fetch(*range(8, 12))
     parts = pieces_of(attn_own, attn_other)
     back = sum(dot(p, w[...]) for p, w in zip(parts, attn)).astype(bf16)
     d_mixed[:, 0:384] = dot(row_move(), back).astype(bf16)
@@ -587,33 +722,37 @@
     d_mixed[:, 384:480] = dot(back, hot(source - 160, target))[:, 0:96].astype(bf16)
 
 
-def middle(mixed_columns, stream, vectors, upstream, targets, target_columns, qkv, attn, expand, reduce):
-    big = (*qkv, *attn, *expand, *reduce)
-    scratch = [jax.ShapeDtypeStruct((512, 256), bf16)] * 4 + list(big[4:])
-    args = (mixed_columns, stream, vectors, upstream, targets, target_columns)
-    half = shape(TOKENS, HALF)
+def fall(here, d_upward, mid, upstream, vectors, offsets, expand, qkv, attn):
+    big = (*expand, *qkv, *attn)
+    args = (d_upward, mid, upstream, vectors, offsets)
     outs = (
-        (shape(TOKENS, D), shape(TOKENS, D, f32))
-        + (half,) * 6
-        + (shape(TOKENS, D), shape(TOKENS, 512), shape(TOKENS, 480), shape(8, D, f32))
-    )
-    return call(
-        middle_kernel,
+        shape(TOKENS, D, f32),
+        shape(TOKENS, HALF),
+        shape(TOKENS, HALF),
+        shape(TOKENS, 480),
+        shape(8, D, f32),
+    )
+    return call(
+        fall_kernel,
         outs,
-        vmem=60,
-        flops=25e9,
+        flops=5e9,
         grid=(1,),
-        in_specs=[whole(v) for v in args] + [pl.BlockSpec(memory_space=pl.ANY)] * 16,
+        in_specs=[pl.BlockSpec(memory_space=pltpu.SMEM)]
+        + [whole(v) for v in args]
+        + [pl.BlockSpec(memory_space=pl.ANY)] * 12,
         out_specs=tuple(whole(v) for v in outs),
-        scratch_shapes=fetched(scratch)
-        + [pltpu.VMEM((TOKENS, D), f32)] * 3
-        + [pltpu.VMEM((TOKENS, 2 * HALF), bf16), pltpu.VMEM((TOKENS, D), bf16)],
-    )(*args, *big)
+        scratch_shapes=fetched(list(expand) + REST + list(attn))
+        + [
+            pltpu.VMEM((TOKENS, D), f32),
+            pltpu.VMEM((TOKENS, 2 * HALF), bf16),
+            pltpu.VMEM((TOKENS, D), bf16),
+        ],
+    )(here, *args, *big)
 
 
 def last_kernel(*refs):
-    small, big, outs, scratch = split_refs(refs, 9, 4, 4, len(refs) - 17)
-    level, d_packed, stream, d_mid, vectors, sums, target_columns, shard_column, marks = small
+    small, big, outs, scratch = split_refs(refs, 10, 4, 4, len(refs) - 18)
+    here, level, d_packed, stream, d_mid, vectors, sums, offsets, shard_column, marks = small
     d_stream, low_a, low_b, spread = outs
     fetch = Fetch(big, scratch[:4], scratch[4])
     work, wide, totals = scratch[5:]
@@ -621,7 +760,7 @@
     for k in range(4):
         wide[:, 512 * k : 512 * k + 512] = cols_dot(d_packed[:, 0:1440], weight[k][:, 0:1440]).astype(bf16)
     wide[...] = dot(row_move(True), wide[...]).astype(bf16)
-    unshuffle(wide, target_columns, 0, work)
+    unshuffle(here, offsets, 0, wide, work)
     totals[...] = jnp.zeros(totals.shape, f32)
 
     def rows(span):
@@ -649,16 +788,15 @@
     spread[...] = cols_dot(hot(shard_column[:, 2:3], marks[0:1, :]), repeated).astype(bf16)
 
 
-def last(level, d_packed, stream, d_mid, vectors, sums, target_columns, shard_column, marks, qkv):
-    args = (d_packed, stream, d_mid, vectors, sums, target_columns, shard_column, marks)
+def last(here, level, d_packed, stream, d_mid, vectors, sums, offsets, shard_column, marks, qkv):
+    args = (d_packed, stream, d_mid, vectors, sums, offsets, shard_column, marks)
     outs = (shape(TOKENS, D, f32), shape(TOKENS, 1024), shape(TOKENS, 896), shape(SHARDS, 128))
     return call(
         last_kernel,
         outs,
-        vmem=48,
         flops=6e9,
         grid=(1,),
-        in_specs=[pl.BlockSpec(memory_space=pltpu.SMEM)]
+        in_specs=[pl.BlockSpec(memory_space=pltpu.SMEM)] * 2
         + [whole(v) for v in args]
         + [pl.BlockSpec(memory_space=pl.ANY)] * 4,
         out_specs=tuple(whole(v) for v in outs),
@@ -668,7 +806,7 @@
             pltpu.VMEM((TOKENS, 2 * HALF), bf16),
             pltpu.VMEM((8, D), f32),
         ],
-    )(level, *args, *qkv)
+    )(here, level, *args, *qkv)
 
 
 def finish_kernel(kept0, got0, kept1, got1, kept2, got2, *outs):
@@ -720,7 +858,8 @@
 ):
     yl, co, yh, z, x = (lax.axis_index(name) for name in AXES)
     me = yl * 64 + co * 32 + yh * 16 + z * 4 + x
-    targets, target_columns, shard_column, codes = places(jnp.stack((me, co)), cond_codes)
+    here = jnp.stack((me, co))
+    targets, offsets, shard_column, codes = places(here, cond_codes)
     shards = prepare(
         qkv_weight,
         attn_out_weight.T,
@@ -741,8 +880,8 @@
         return [v for (v,) in lists]
 
     small = singles(join(shards, exchanged(shards, 0)))
-    small, (targets, target_columns, shard_column, codes) = lax.optimization_barrier(
-        (small, (targets, target_columns, shard_column, codes))
+    small, (targets, offsets, shard_column, codes) = lax.optimization_barrier(
+        (small, (targets, offsets, shard_column, codes))
     )
     for step in (1, 2):
         small = singles(join(small, exchanged(small, step)))
@@ -760,7 +899,7 @@
     rests = exchanged(second, 5)
 
     stream, first_own, first_other, packed, vectors = embed(
-        level_ids, hidden_in[0], codes, targets, shard_column, marks, table_a, table_b, qkv
+        here, level_ids, hidden_in[0], codes, targets, offsets, shard_column, marks, table_a, table_b, qkv
     )
 
     def over_blocks(value):
@@ -772,30 +911,28 @@
     mixed = over_blocks(mixed)
     attn, expand, reduce = [(h, r, swap_cores(h), swap_cores(r)) for h, r in zip(second, rests)]
     upstream = grad_out[0]
-    (
-        block_out,
-        d_mid,
-        second_own,
-        second_other,
-        active_own,
-        active_other,
-        attn_own,
-        attn_other,
-        d_upward,
-        mixed,
-        d_mixed,
-        sums,
-    ) = middle(mixed, stream, vectors, upstream, targets, target_columns, qkv, attn, expand, reduce)
+    upstream_got = swap_cores(upstream)
+    mixed, mid, second_own, second_other, active_own, active_other, slope = rise(
+        here, mixed, stream, vectors, offsets, qkv, attn, expand
+    )
+    reduce_grad = outer(2, active_own, swap_cores(active_other), upstream, upstream_got)
+    second_got, mixed_got = swap_cores(second_other), swap_cores(mixed)
+    active_own, reduce_grad = lax.optimization_barrier((active_own, reduce_grad))
+    reduce_got = exchange(reduce_grad[1], ORDERS[2], 5)
+    block_out, d_upward = turn(
+        here, mid, active_own, active_other, slope, upstream, offsets, reduce
+    )
+    expand_grad = outer(1, second_own, second_got, d_upward, swap_cores(d_upward))
+    d_upward, expand_grad = lax.optimization_barrier((d_upward, expand_grad))
+    expand_got = exchange(expand_grad[1], ORDERS[1], 5)
+    d_mid, attn_own, attn_other, d_mixed, sums = fall(
+        here, d_upward, mid, upstream, vectors, offsets, expand, qkv, attn
+    )
     d_mixed = over_blocks(d_mixed)
-    early = [
-        outer(own, swap_cores(other), right, swap_cores(right))
-        for own, other, right in (
-            (attn_own, attn_other, mixed),
-            (second_own, second_other, d_upward),
-            (active_own, active_other, upstream),
-        )
-    ]
-    early_got = exchanged([sent for _, sent in early], 5)
+    attn_grad = outer(0, attn_own, swap_cores(attn_other), mixed, mixed_got)
+    attn_got = exchange(attn_grad[1], ORDERS[0], 5)
+    early = (attn_grad, expand_grad, reduce_grad)
+    early_got = (attn_got, expand_got, reduce_got)
     first_got = swap_cores(first_other)
     codes_got = swap_cores(codes)
 
@@ -803,15 +940,15 @@
     early = add_halves([[(kept, got)] for (kept, _), got in zip(early, early_got)])
     d_packed, early = lax.optimization_barrier((d_packed, early))
     early_got = exchanged([sent for _, sent in early], 4)
-    qkv_grad = outer(first_own, first_got, d_packed, swap_cores(d_packed))
+    qkv_grad = outer(0, first_own, first_got, d_packed, swap_cores(d_packed))
     d_packed, qkv_grad = lax.optimization_barrier((d_packed, qkv_grad))
 
     d_stream, low_a, low_b, small = last(
-        level_ids, d_packed, stream, d_mid, vectors, sums, target_columns, shard_column, marks, qkv
+        here, level_ids, d_packed, stream, d_mid, vectors, sums, offsets, shard_column, marks, qkv
     )
     small = small[:64] + swap_cores(small[64:])
-    grad_a = outer(codes, codes_got, low_a, swap_cores(low_a), 3, targets)
-    grad_b = outer(codes, codes_got, low_b, swap_cores(low_b), 4, targets, small)
+    grad_a = table_outer(3, codes, codes_got, low_a, swap_cores(low_a), targets)
+    grad_b = table_outer(4, codes, codes_got, low_b, swap_cores(low_b), targets, small)
     late = [qkv_grad, grad_a, grad_b]
     late_got = exchanged([sent for _, sent in late], 5)
     late = add_halves([[(kept, got)] for (kept, _), got in zip(late, late_got)])

time: 431 us -> 462 us (1.072)
  Pallas kernels: 113 us -> 173 us
  waiting for transfers between devices: 182 us -> 165 us
  starting transfers between devices: 95.2 us -> 87.9 us
  local copies, waits for them, and re-layouts: 30 us -> 23.5 us
    pallas_call x26 -> x28, Pallas kernels: 113 us -> 173 us  [run(): pl.pallas_call(kernel, out_shape=out_shape, compiler_params=params, cost_...]
    all_to_all x4, waiting for transfers between devices: 45 us -> 33.8 us  [over_blocks(): return lax.all_to_all(value, BLK, split_axis=0, concat_axis=0, tiled=True)]
    unnamed x130 -> x134, local copies, waits for them, and re-layouts: 30 us -> 22.8 us
    all_to_all x4, starting transfers between devices: 23.2 us -> 18 us  [over_blocks(): return lax.all_to_all(value, BLK, split_axis=0, concat_axis=0, tiled=True)]
    ppermute x24, waiting for transfers between devices: 15.2 us -> 10.4 us  [swap_cores(): return lax.ppermute(value, AXES, [(i, i ^ CORE_BIT) for i in range(SHARDS)])]
  transfers between devices with their start and end apart: 76 -> 76, of which waited for: 33 -> 34; matrix products, arithmetic and copies ran while one was open for 0% -> 1% of each run, Pallas kernels for 21% -> 22%
where the time goes in v2:
time: 462 us; the launch traced here: 453 us
  Pallas kernels  173 us (37%)
  waiting for transfers between devices  165 us (36%)
  starting transfers between devices  87.9 us (19%)
  local copies, waits for them, and re-layouts  23.5 us (5%)
    pallas_call x28, Pallas kernels, run(): pl.pallas_call(kernel, out_shape=out_shape, compiler_params=params, cost_...  173 us
    ppermute x48, waiting for transfers between devices, exchange(): return lax.ppermute(value, AXES, pairs)  121 us
    ppermute x48, starting transfers between devices, exchange(): return lax.ppermute(value, AXES, pairs)  63.4 us
    all_to_all x4, waiting for transfers between devices, over_blocks(): return lax.all_to_all(value, BLK, split_axis=0, concat_axis=0, tiled=True)  33.8 us
    unnamed x134, local copies, waits for them, and re-layouts  22.8 us
    all_to_all x4, starting transfers between devices, over_blocks(): return lax.all_to_all(value, BLK, split_axis=0, concat_axis=0, tiled=True)  18 us
    ppermute x24, waiting for transfers between devices, swap_cores(): return lax.ppermute(value, AXES, [(i, i ^ CORE_BIT) for i in range(SHARDS)])  10.4 us
  transfers between devices with their start and end apart: 76, of which 34 were waited for; matrix products, arithmetic and copies ran while one was open for 1% of the time, Pallas kernels for 22%

profile of v2, /device:TPU:0, one launch (start us, length us, event | category | flops | bytes accessed | tf_op | source)
XLA Modules:
  0.0 453.4 jit_solution(2542860456665990465)
XLA Ops:
  45.1 9.5 %collective-permute-done.9.refs_1_ = bf16[128,1920]{1,0:T(8,128)(2,1)S(1)} collective-permute-done((bf16[128,1920]{1,0:T(8,128)(2,1)}, bf16[128,1920]{1,0:T(8,128)(2,1)S(1)}, u32[]{:S(2)}, u32[]{:S(2)}) %collective-permute-start.9) | collective-permute-done | bytes 491552 | tf_op jit(solution)/shard_map/ppermute | solution.py:38
  62.6 8.4 %collective-permute-done.14.refs_5_ = bf16[256,896]{1,0:T(8,128)(2,1)S(1)} collective-permute-done((bf16[256,896]{1,0:T(8,128)(2,1)}, bf16[256,896]{1,0:T(8,128)(2,1)S(1)}, u32[]{:S(2)}, u32[]{:S(2)}) %collective-permute-start.14) | collective-permute-done | bytes 458784 | tf_op jit(solution)/shard_map/ppermute | solution.py:38
  84.6 5.4 %collective-permute-done.24.refs_1_ = bf16[256,384]{1,0:T(8,128)(2,1)S(1)} collective-permute-done((bf16[256,384]{1,0:T(8,128)(2,1)S(1)}, bf16[256,384]{1,0:T(8,128)(2,1)S(1)}, u32[]{:S(2)}, u32[]{:S(2)}) %collective-permute-start.24) | collective-permute-done | bytes 196640 | tf_op jit(solution)/shard_map/ppermute | solution.py:38
  90.3 6.1 %collective-permute-done.21.refs_13_ = bf16[512,896]{1,0:T(8,128)(2,1)} collective-permute-done((bf16[512,896]{1,0:T(8,128)(2,1)}, bf16[512,896]{1,0:T(8,128)(2,1)}, u32[]{:S(2)}, u32[]{:S(2)}) %collective-permute-start.21) | collective-permute-done | bytes 917536 | tf_op jit(solution)/shard_map/ppermute | solution.py:38
  96.5 6.3 %collective-permute-done.15.refs_17_.refs_6_.refs_11_ = bf16[512,1536]{1,0:T(8,128)(2,1)S(1)} collective-permute-done((bf16[512,1536]{1,0:T(8,128)(2,1)}, bf16[512,1536]{1,0:T(8,128)(2,1)S(1)}, u32[]{:S(2)}, u32[]{:S(2)}) %collective-permute-start.15) | collective-permute-done | bytes 1572896 | tf_op jit(solution)/shard_map/ppermute | solution.py:38
  121.7 14.5 %shard_map.239 = (f32[256,1920]{1,0:T(8,128)}, bf16[256,1024]{1,0:T(8,128)(2,1)}, bf16[256,1024]{1,0:T(8,128)(2,1)}, bf16[256,1440]{1,0:T(8,128)(2,1)}, f32[8,1920]{1,0:T(8,128)}) custom-call(s32[2]{0:T(128)} %pad_add_fusion.here.refs_0_, s32[1]{0:T(128)S(6)} %copy.26.refs_1_, bf16[256,1920]{1,0:T(8,128)(2,1)} %bitcast.32, ...), custom_call_target="tpu_custom_call" | custom-call | flops 8000000000 | bytes 19046412 | tf_op jit(solution)/shard_map/pallas_call | solution.py:52
  144.6 12.4 %all-to-all-done = bf16[32,8,1440]{2,1,0:T(8,128)(2,1)S(1)} async-done(((bf16[32,8,1440]{2,1,0:T(8,128)(2,1)}), bf16[32,8,1440]{2,1,0:T(8,128)(2,1)S(1)}, u32[]{:S(2)}, u32[]{:S(2)}) %all-to-all-start) | async-done | bytes 737312 | tf_op jit(solution)/shard_map/all_to_all | solution.py:906
  170.3 10.7 %all-to-all-done.1 = bf16[32,8,480]{2,1,0:T(8,128)(2,1)S(1)} async-done(((bf16[32,8,480]{2,1,0:T(8,128)(2,1)}), bf16[32,8,480]{2,1,0:T(8,128)(2,1)S(1)}, u32[]{:S(2)}, u32[]{:S(2)}) %all-to-all-start.1) | async-done | bytes 245792 | tf_op jit(solution)/shard_map/all_to_all | solution.py:906
  181.8 19.3 %shard_map.241 = (bf16[256,512]{1,0:T(8,128)(2,1)}, f32[256,1920]{1,0:T(8,128)}, bf16[256,1024]{1,0:T(8,128)(2,1)}, bf16[256,1024]{1,0:T(8,128)(2,1)}, bf16[256,...) custom-call(s32[2]{0:T(128)} %pad_add_fusion.here.refs_0_, bf16[256,480]{1,0:T(8,128)(2,1)} %bitcast.29, ...), custom_call_target="tpu_custom_call" | custom-call | flops 6000000000 | bytes 24301576 | tf_op jit(solution)/shard_map/pallas_call | solution.py:52
  204.7 6.8 %shard_map.242 = (bf16[512,1920]{1,0:T(8,128)(2,1)}, bf16[512,1920]{1,0:T(8,128)(2,1)}) custom-call(bf16[256,1024]{1,0:T(8,128)(2,1)} %get-tuple-element.232.left.refs_2_, bf16[256,1024]{1,0:T(8,128)(2,1)} %copy-done.62, bf16[256,1920]{1,0:T(8,128)(2,1)} %bitcast.22, bf16[256,1920]{1,0:T(8,128)(2,1)} %copy-done.51), custom_call_target="tpu_custom_call" | custom-call | flops 2013265920 | bytes 6946816 | tf_op jit(solution)/shard_map/pallas_call | solution.py:52
  211.5 16.3 %shard_map.243 = (bf16[256,1920]{1,0:T(8,128)(2,1)}, bf16[256,1920]{1,0:T(8,128)(2,1)}) custom-call(s32[2]{0:T(128)} %pad_add_fusion.here.refs_0_, f32[256,1920]{1,0:T(8,128)} %get-tuple-element.227.refs_1_.refs_2_, bf16[256,1024]{1,0:T(8,128)(2,1)} %get-tuple-element.232.left.refs_2_, bf16[256,1024]{1,0:T(8,128)(2,1)} %get-tuple-element.229.refs_3_, ...), custom_call_target="tpu_custom_call" | custom-call | flops 6000000000 | bytes 15802376 | tf_op jit(solution)/shard_map/pallas_call | solution.py:52
  232.3 6.8 %shard_map.244 = (bf16[512,1920]{1,0:T(8,128)(2,1)}, bf16[512,1920]{1,0:T(8,128)(2,1)}) custom-call(bf16[256,1024]{1,0:T(8,128)(2,1)} %get-tuple-element.237.left, bf16[256,1024]{1,0:T(8,128)(2,1)} %copy-done.60, bf16[256,1920]{1,0:T(8,128)(2,1)} %get-tuple-element.241.right.refs_1_, bf16[256,1920]{1,0:T(8,128)(2,1)} %copy-done.52), custom_call_target="tpu_custom_call" | custom-call | flops 2013265920 | bytes 6946816 | tf_op jit(solution)/shard_map/pallas_call | solution.py:52
  240.6 18.7 %shard_map.245 = (f32[256,1920]{1,0:T(8,128)}, bf16[256,1024]{1,0:T(8,128)(2,1)}, bf16[256,1024]{1,0:T(8,128)(2,1)}, bf16[256,480]{1,0:T(8,128)(2,1)}, f32[8,1920]{1,0:T(8,128)}) custom-call(s32[2]{0:T(128)} %pad_add_fusion.here.refs_0_, bf16[256,1920]{1,0:T(8,128)(2,1)} %get-tuple-element.241.right.refs_1_, f32[256,1920]{1,0:T(8,128)} %get-tuple-element.227.refs_1_.refs_2_, ...), custom_call_target="tpu_custom_call" | custom-call | flops 5000000000 | bytes 23052296 | tf_op jit(solution)/shard_map/pallas_call | solution.py:52
  264.5 10.7 %all-to-all-done.2 = bf16[32,8,480]{2,1,0:T(8,128)(2,1)S(1)} async-done(((bf16[32,8,480]{2,1,0:T(8,128)(2,1)}), bf16[32,8,480]{2,1,0:T(8,128)(2,1)S(1)}, u32[]{:S(2)}, u32[]{:S(2)}) %all-to-all-start.2) | async-done | bytes 245792 | tf_op jit(solution)/shard_map/all_to_all | solution.py:906
  291.4 10.2 %collective-permute-done.42.refs_2_.refs_3_ = bf16[512,512]{1,0:T(8,128)(2,1)S(1)} collective-permute-done((bf16[512,512]{1,0:T(8,128)(2,1)}, bf16[512,512]{1,0:T(8,128)(2,1)S(1)}, u32[]{:S(2)}, u32[]{:S(2)}) %collective-permute-start.42) | collective-permute-done | bytes 524320 | tf_op jit(solution)/shard_map/ppermute | solution.py:38
  302.4 5.6 %shard_map.248 = (bf16[256,512]{1,0:T(8,128)(2,1)}, bf16[256,512]{1,0:T(8,128)(2,1)}, bf16[256,1920]{1,0:T(8,128)(2,1)}, bf16[256,1920]{1,0:T(8,128)(2,1)}, bf16...) custom-call(bf16[512,512]{1,0:T(8,128)(2,1)} %get-tuple-element.246.refs_0_.refs_1_, ...), custom_call_target="tpu_custom_call" | custom-call | bytes 22282240 | tf_op jit(solution)/shard_map/pallas_call | solution.py:52
  312.2 7.3 %shard_map.249 = (bf16[512,1536]{1,0:T(8,128)(2,1)}, bf16[512,1536]{1,0:T(8,128)(2,1)}) custom-call(bf16[256,1024]{1,0:T(8,128)(2,1)} %get-tuple-element.259.left, bf16[256,1024]{1,0:T(8,128)(2,1)} %copy-done.61, bf16[256,1536]{1,0:T(8,128)(2,1)} %bitcast.26, bf16[256,1536]{1,0:T(8,128)(2,1)} %copy-done.55), custom_call_target="tpu_custom_call" | custom-call | flops 1610612736 | bytes 5767168 | tf_op jit(solution)/shard_map/pallas_call | solution.py:52
  319.5 14.1 %shard_map.250 = (f32[256,1920]{1,0:T(8,128)}, bf16[256,1024]{1,0:T(8,128)(2,1)}, bf16[256,896]{1,0:T(8,128)(2,1)}, bf16[128,128]{1,0:T(8,128)(2,1)}) custom-call(s32[2]{0:T(128)} %pad_add_fusion.here.refs_0_, s32[1]{0:T(128)S(6)} %copy.26.refs_1_, bf16[256,1536]{1,0:T(8,128)(2,1)} %bitcast.27, f32[256,1920]{1,0:T(8,128)} %get-tuple-element.223.refs_2_.refs_3_, ...), custom_call_target="tpu_custom_call" | custom-call | flops 6000000000 | bytes 14142476 | tf_op jit(solution)/shard_map/pallas_call | solution.py:52
  353.8 9.9 %collective-permute-done.54.refs_10_.refs_11_ = bf16[512,1024]{1,0:T(8,128)(2,1)S(1)} collective-permute-done((bf16[512,1024]{1,0:T(8,128)(2,1)}, bf16[512,1024]{1,0:T(8,128)(2,1)S(1)}, u32[]{:S(2)}, u32[]{:S(2)}) %collective-permute-start.54) | collective-permute-done | bytes 1048608 | tf_op jit(solution)/shard_map/ppermute | solution.py:38
  364.7 11.5 %collective-permute-done.51.refs_6_.refs_7_ = bf16[512,1024]{1,0:T(8,128)(2,1)S(1)} collective-permute-done((bf16[512,1024]{1,0:T(8,128)(2,1)}, bf16[512,1024]{1,0:T(8,128)(2,1)S(1)}, u32[]{:S(2)}, u32[]{:S(2)}) %collective-permute-start.51) | collective-permute-done | bytes 1048608 | tf_op jit(solution)/shard_map/ppermute | solution.py:38
  383.7 8.3 %collective-permute-done.57.refs_14_.refs_15_ = bf16[256,1024]{1,0:T(8,128)(2,1)S(1)} collective-permute-done((bf16[256,1024]{1,0:T(8,128)(2,1)}, bf16[256,1024]{1,0:T(8,128)(2,1)S(1)}, u32[]{:S(2)}, u32[]{:S(2)}) %collective-permute-start.57) | collective-permute-done | bytes 524320 | tf_op jit(solution)/shard_map/ppermute | solution.py:38
  395.6 5.4 %shard_map.254 = (bf16[128,2048]{1,0:T(8,128)(2,1)}, bf16[128,2048]{1,0:T(8,128)(2,1)}, bf16[128,2944]{1,0:T(8,128)(2,1)}, bf16[128,2944]{1,0:T(8,128)(2,1)}, bf...) custom-call(bf16[256,512]{1,0:T(8,128)(2,1)} %get-tuple-element.267.refs_0_.refs_1_, ...), custom_call_target="tpu_custom_call" | custom-call | bytes 20316160 | tf_op jit(solution)/shard_map/pallas_call | solution.py:52
  406.8 8.7 %collective-permute-done.60.refs_2_.refs_3_ = bf16[128,2048]{1,0:T(8,128)(2,1)S(1)} collective-permute-done((bf16[128,2048]{1,0:T(8,128)(2,1)}, bf16[128,2048]{1,0:T(8,128)(2,1)S(1)}, u32[]{:S(2)}, u32[]{:S(2)}) %collective-permute-start.60) | collective-permute-done | bytes 524320 | tf_op jit(solution)/shard_map/ppermute | solution.py:38
  421.1 6.2 %collective-permute-done.63.refs_2_.refs_3_ = bf16[64,2048]{1,0:T(8,128)(2,1)S(1)} collective-permute-done((bf16[64,2048]{1,0:T(8,128)(2,1)}, bf16[64,2048]{1,0:T(8,128)(2,1)S(1)}, u32[]{:S(2)}, u32[]{:S(2)}) %collective-permute-start.63) | collective-permute-done | bytes 262176 | tf_op jit(solution)/shard_map/ppermute | solution.py:38
  (293 shorter events, 212.3 us)
Async XLA Ops:
  78.8 23.9 %collective-permute-start.15 = (bf16[512,1536]{1,0:T(8,128)(2,1)}, bf16[512,1536]{1,0:T(8,128)(2,1)S(1)}, u32[]{:S(2)}, u32[]{:S(2)}) collective-permute-start(bf16[512,1536]{1,0:T(8,128)(2,1)} %get-tuple-element.214.refs_16_.refs_5_.refs_10_), channel_id=1, source_target_pairs={{0,80},{1,81},{2,82},{3,83},{4,84},{5,85},{6,86},{7,87},{8,88},{9,... | collective-permute-start | bytes 4718600 | tf_op jit(solution)/shard_map/ppermute | solution.py:38
  82.3 27.6 %collective-permute-start.18 = (bf16[512,1024]{1,0:T(8,128)(2,1)}, bf16[512,1024]{1,0:T(8,128)(2,1)}, u32[]{:S(2)}, u32[]{:S(2)}) collective-permute-start(bf16[512,1024]{1,0:T(8,128)(2,1)} %get-tuple-element.206.refs_8_), channel_id=1, source_target_pairs={{0,3},{1,2},{2,1},{3,0},{4,7},{5,6},{6,5},{7,4},{8,11},{9,10},{10,... | collective-permute-start | bytes 3145736 | tf_op jit(solution)/shard_map/ppermute | solution.py:38
  90.0 17.6 %collective-permute-start.25 = (bf16[256,1920]{1,0:T(8,128)(2,1)S(1)}, bf16[256,1920]{1,0:T(8,128)(2,1)S(1)}, u32[]{:S(2)}, u32[]{:S(2)}) collective-permute-start(bf16[256,1920]{1,0:T(8,128)(2,1)S(1)} %copy-done.20), channel_id=1, source_target_pairs={{0,1},{1,0},{2,3},{3,2},{4,5},{5,4},{6,7},{7,6},{8,9},{9,8},{10,11... | collective-permute-start | bytes 2949128 | tf_op jit(solution)/shard_map/ppermute | solution.py:38
  96.4 19.8 %collective-permute-start.16 = (bf16[512,1536]{1,0:T(8,128)(2,1)}, bf16[512,1536]{1,0:T(8,128)(2,1)S(1)}, u32[]{:S(2)}, u32[]{:S(2)}) collective-permute-start(bf16[512,1536]{1,0:T(8,128)(2,1)} %get-tuple-element.214.refs_16_.refs_5_.refs_10_), channel_id=1, source_target_pairs={{0,32},{1,33},{2,34},{3,35},{4,36},{5,37},{6,38},{7,39},{8,40},{9,... | collective-permute-start | bytes 4718600 | tf_op jit(solution)/shard_map/ppermute | solution.py:42
  116.2 44.3 %collective-permute-start.28 = (bf16[512,1920]{1,0:T(8,128)(2,1)}, bf16[512,1920]{1,0:T(8,128)(2,1)}, u32[]{:S(2)}, u32[]{:S(2)}) collective-permute-start(bf16[512,1920]{1,0:T(8,128)(2,1)} %get-tuple-element.220.refs_13_.refs_6_), channel_id=1, source_target_pairs={{0,3},{1,2},{2,1},{3,0},{4,7},{5,6},{6,5},{7,4},{8,11},{9,10},{10,... | collective-permute-start | bytes 5898248 | tf_op jit(solution)/shard_map/ppermute | solution.py:38
  119.2 41.4 %collective-permute-start.29 = (bf16[512,1920]{1,0:T(8,128)(2,1)}, bf16[512,1920]{1,0:T(8,128)(2,1)}, u32[]{:S(2)}, u32[]{:S(2)}) collective-permute-start(bf16[512,1920]{1,0:T(8,128)(2,1)} %get-tuple-element.221.refs_7_), channel_id=1, source_target_pairs={{0,12},{1,13},{2,14},{3,15},{4,8},{5,9},{6,10},{7,11},{8,4},{9,5},... | collective-permute-start | bytes 5898248 | tf_op jit(solution)/shard_map/ppermute | solution.py:38
  136.2 20.7 %all-to-all-start = ((bf16[32,8,1440]{2,1,0:T(8,128)(2,1)}), bf16[32,8,1440]{2,1,0:T(8,128)(2,1)S(1)}, u32[]{:S(2)}, u32[]{:S(2)}) async-start(bf16[32,8,1440]{2,1,0:T(8,128)(2,1)} %bitcast.28), calls=%async_computation | async-start | bytes 1572864 | tf_op jit(solution)/shard_map/all_to_all | solution.py:906
  141.0 19.6 %collective-permute-start.27 = (bf16[512,384]{1,0:T(8,128)(2,1)S(1)}, bf16[512,384]{1,0:T(8,128)(2,1)S(1)}, u32[]{:S(2)}, u32[]{:S(2)}) collective-permute-start(bf16[512,384]{1,0:T(8,128)(2,1)S(1)} %copy-done.32), channel_id=1, source_target_pairs={{0,80},{1,81},{2,82},{3,83},{4,84},{5,85},{6,86},{7,87},{8,88},{9,... | collective-permute-start | bytes 1179656 | tf_op jit(solution)/shard_map/ppermute | solution.py:38
  144.6 25.7 %collective-permute-start.32 = (bf16[512,1920]{1,0:T(8,128)(2,1)S(1)}, bf16[512,1920]{1,0:T(8,128)(2,1)}, u32[]{:S(2)}, u32[]{:S(2)}) collective-permute-start(bf16[512,1920]{1,0:T(8,128)(2,1)S(1)} %copy-done.12), channel_id=1, source_target_pairs={{0,32},{1,33},{2,34},{3,35},{4,36},{5,37},{6,38},{7,39},{8,40},{9,... | collective-permute-start | bytes 5898248 | tf_op jit(solution)/shard_map/ppermute | solution.py:42
  160.6 20.4 %collective-permute-start.33 = (bf16[512,1920]{1,0:T(8,128)(2,1)}, bf16[512,1920]{1,0:T(8,128)(2,1)}, u32[]{:S(2)}, u32[]{:S(2)}) collective-permute-start(bf16[512,1920]{1,0:T(8,128)(2,1)} %collective-permute-done.28.refs_14_.refs_7_), channel_id=1, source_target_pairs={{0,32},{1,33},{2,34},{3,35},{4,36},{5,37},{6,38},{7,39},{8,40},{9,... | collective-permute-start | bytes 5898248 | tf_op jit(solution)/shard_map/ppermute | solution.py:42
  161.2 50.3 %collective-permute-start.36 = (bf16[512,1920]{1,0:T(8,128)(2,1)}, bf16[512,1920]{1,0:T(8,128)(2,1)}, u32[]{:S(2)}, u32[]{:S(2)}) collective-permute-start(bf16[512,1920]{1,0:T(8,128)(2,1)} %get-tuple-element.221.refs_7_), channel_id=1, source_target_pairs={{0,32},{1,33},{2,34},{3,35},{4,36},{5,37},{6,38},{7,39},{8,40},{9,... | collective-permute-start | bytes 5898248 | tf_op jit(solution)/shard_map/ppermute | solution.py:42
  161.3 50.2 %collective-permute-start.37 = (bf16[512,1920]{1,0:T(8,128)(2,1)}, bf16[512,1920]{1,0:T(8,128)(2,1)}, u32[]{:S(2)}, u32[]{:S(2)}) collective-permute-start(bf16[512,1920]{1,0:T(8,128)(2,1)} %collective-permute-done.29.refs_8_), channel_id=1, source_target_pairs={{0,32},{1,33},{2,34},{3,35},{4,36},{5,37},{6,38},{7,39},{8,40},{9,... | collective-permute-start | bytes 5898248 | tf_op jit(solution)/shard_map/ppermute | solution.py:42
  170.2 31.5 %collective-permute-start.35 = (bf16[256,1920]{1,0:T(8,128)(2,1)}, bf16[256,1920]{1,0:T(8,128)(2,1)S(1)}, u32[]{:S(2)}, u32[]{:S(2)}) collective-permute-start(bf16[256,1920]{1,0:T(8,128)(2,1)} %bitcast.21), channel_id=1, source_target_pairs={{0,32},{1,33},{2,34},{3,35},{4,36},{5,37},{6,38},{7,39},{8,40},{9,... | collective-permute-start | bytes 2949128 | tf_op jit(solution)/shard_map/ppermute | solution.py:42
  228.4 63.0 %collective-permute-start.44 = (bf16[512,1920]{1,0:T(8,128)(2,1)}, bf16[512,1920]{1,0:T(8,128)(2,1)S(1)}, u32[]{:S(2)}, u32[]{:S(2)}) collective-permute-start(bf16[512,1920]{1,0:T(8,128)(2,1)} %get-tuple-element.251), channel_id=1, source_target_pairs={{0,12},{1,13},{2,14},{3,15},{4,8},{5,9},{6,10},{7,11},{8,4},{9,5},... | collective-permute-start | bytes 5898248 | tf_op jit(solution)/shard_map/ppermute | solution.py:38
  239.1 62.5 %collective-permute-start.43 = (bf16[512,1920]{1,0:T(8,128)(2,1)}, bf16[512,1920]{1,0:T(8,128)(2,1)}, u32[]{:S(2)}, u32[]{:S(2)}) collective-permute-start(bf16[512,1920]{1,0:T(8,128)(2,1)} %get-tuple-element.249), channel_id=1, source_target_pairs={{0,3},{1,2},{2,1},{3,0},{4,7},{5,6},{6,5},{7,4},{8,11},{9,10},{10,... | collective-permute-start | bytes 5898248 | tf_op jit(solution)/shard_map/ppermute | solution.py:38
  259.4 23.9 %collective-permute-start.40 = (bf16[256,1024]{1,0:T(8,128)(2,1)}, bf16[256,1024]{1,0:T(8,128)(2,1)S(1)}, u32[]{:S(2)}, u32[]{:S(2)}) collective-permute-start(bf16[256,1024]{1,0:T(8,128)(2,1)} %get-tuple-element.244), channel_id=1, source_target_pairs={{0,32},{1,33},{2,34},{3,35},{4,36},{5,37},{6,38},{7,39},{8,40},{9,... | collective-permute-start | bytes 1572872 | tf_op jit(solution)/shard_map/ppermute | solution.py:42
  264.2 19.1 %collective-permute-start.41 = (bf16[256,512]{1,0:T(8,128)(2,1)S(1)}, bf16[256,512]{1,0:T(8,128)(2,1)}, u32[]{:S(2)}, u32[]{:S(2)}) collective-permute-start(bf16[256,512]{1,0:T(8,128)(2,1)S(1)} %copy-done.64), channel_id=1, source_target_pairs={{0,32},{1,33},{2,34},{3,35},{4,36},{5,37},{6,38},{7,39},{8,40},{9,... | collective-permute-start | bytes 786440 | tf_op jit(solution)/shard_map/ppermute | solution.py:42
  279.2 28.8 %all-to-all-start.3 = ((bf16[32,8,1536]{2,1,0:T(8,128)(2,1)}), bf16[32,8,1536]{2,1,0:T(8,128)(2,1)S(1)}, u32[]{:S(2)}, u32[]{:S(2)}) async-start(bf16[32,8,1536]{2,1,0:T(8,128)(2,1)} %bitcast.18), calls=%async_computation.3 | async-start | bytes 1572864 | tf_op jit(solution)/shard_map/all_to_all | solution.py:906
  334.2 42.1 %collective-permute-start.48 = (bf16[512,1536]{1,0:T(8,128)(2,1)}, bf16[512,1536]{1,0:T(8,128)(2,1)S(1)}, u32[]{:S(2)}, u32[]{:S(2)}) collective-permute-start(bf16[512,1536]{1,0:T(8,128)(2,1)} %get-tuple-element.270), channel_id=1, source_target_pairs={{0,80},{1,81},{2,82},{3,83},{4,84},{5,85},{6,86},{7,87},{8,88},{9,... | collective-permute-start | bytes 4718600 | tf_op jit(solution)/shard_map/ppermute | solution.py:38
  343.8 19.9 %collective-permute-start.54 = (bf16[512,1024]{1,0:T(8,128)(2,1)}, bf16[512,1024]{1,0:T(8,128)(2,1)S(1)}, u32[]{:S(2)}, u32[]{:S(2)}) collective-permute-start(bf16[512,1024]{1,0:T(8,128)(2,1)} %get-tuple-element.277), channel_id=1, source_target_pairs={{0,12},{1,13},{2,14},{3,15},{4,8},{5,9},{6,10},{7,11},{8,4},{9,5},... | collective-permute-start | bytes 3145736 | tf_op jit(solution)/shard_map/ppermute | solution.py:38
  350.7 25.6 %collective-permute-start.51 = (bf16[512,1024]{1,0:T(8,128)(2,1)}, bf16[512,1024]{1,0:T(8,128)(2,1)S(1)}, u32[]{:S(2)}, u32[]{:S(2)}) collective-permute-start(bf16[512,1024]{1,0:T(8,128)(2,1)} %get-tuple-element.273), channel_id=1, source_target_pairs={{0,3},{1,2},{2,1},{3,0},{4,7},{5,6},{6,5},{7,4},{8,11},{9,10},{10,... | collective-permute-start | bytes 3145736 | tf_op jit(solution)/shard_map/ppermute | solution.py:38
  353.4 30.3 %collective-permute-start.56 = (bf16[256,1920]{1,0:T(8,128)(2,1)}, bf16[256,1920]{1,0:T(8,128)(2,1)}, u32[]{:S(2)}, u32[]{:S(2)}) collective-permute-start(bf16[256,1920]{1,0:T(8,128)(2,1)} %get-tuple-element.281), channel_id=1, source_target_pairs={{0,1},{1,0},{2,3},{3,2},{4,5},{5,4},{6,7},{7,6},{8,9},{9,8},{10,11... | collective-permute-start | bytes 2949128 | tf_op jit(solution)/shard_map/ppermute | solution.py:38
  353.6 30.1 %collective-permute-start.58 = (bf16[256,1920]{1,0:T(8,128)(2,1)}, bf16[256,1920]{1,0:T(8,128)(2,1)}, u32[]{:S(2)}, u32[]{:S(2)}) collective-permute-start(bf16[256,1920]{1,0:T(8,128)(2,1)} %get-tuple-element.285), channel_id=1, source_target_pairs={{0,4},{1,5},{2,6},{3,7},{4,0},{5,1},{6,2},{7,3},{8,12},{9,13},{10,... | collective-permute-start | bytes 2949128 | tf_op jit(solution)/shard_map/ppermute | solution.py:38
  363.7 19.0 %collective-permute-start.47 = (bf16[256,512]{1,0:T(8,128)(2,1)}, bf16[256,512]{1,0:T(8,128)(2,1)S(1)}, u32[]{:S(2)}, u32[]{:S(2)}) collective-permute-start(bf16[256,512]{1,0:T(8,128)(2,1)} %get-tuple-element.268), channel_id=1, source_target_pairs={{0,64},{1,65},{2,66},{3,67},{4,68},{5,69},{6,70},{7,71},{8,72},{9,... | collective-permute-start | bytes 786440 | tf_op jit(solution)/shard_map/ppermute | solution.py:38
  (119 other events, 772.6 us)
